TPU v7x, 256 devices: a whole 4x4x8 slice. The times are simulated.
256 devices in a mesh: var: 32 (over z, y_lo, core), band: 8 (over x, y_hi).
Axes of the slice: x: 4, y: 4 (y_hi: 2, y_lo: 2; y = y_hi * 2 + y_lo), z: 8, core: 2. Of those that a mesh axis runs over, the one named last changes fastest.
Arguments:
- fields: bfloat16 [64, 256, 1024], P('var', None, 'band'), may hold values from -6 to 6
- stem_in: bfloat16 [64, 16, 512], P('var'), may hold values from -1.5 to 1.5
- stem_out: bfloat16 [64, 512, 512], P('var'), may hold values from -0.25 to 0.25
- level_ids: int32 [64], replicated, may hold values from 0 to 127
- level_table: bfloat16 [128, 512], replicated, may hold values from -6 to 6
- latent_query: bfloat16 [4, 512], replicated, may hold values from -100 to 100
- kv_weight: bfloat16 [512, 1024], replicated, may hold values from -0.25 to 0.25
- out_weight: bfloat16 [512, 512], replicated, may hold values from -0.25 to 0.25
- region_ids: int32 [32, 128], replicated, may hold values from 0 to 255, as said below
Outputs:
- latents: bfloat16 [64, 256, 4, 512], P('var', 'band')
- region_means: float32 [256, 4, 512], P(('var', 'band'))
Inputs may be any that keep to these rules, and one draw needn't show every extreme that they name: `region_ids`: every region 0 to 255 holds at least one coarse cell; within each aligned block of 1 coarse rows and 16 coarse columns, every region that occurs occurs exactly 2 times.
All inputs are finite; a program needn't handle non-finite values.
Results may differ from a plain program's by a relative error of at most 0.0065.
Values may be sent and summed in bfloat16 or wider, within the bound.
A program may use at most 64 MiB of HBM per device.

v0:
```python
import jax
import jax.numpy as jnp
from jax import lax
from jax.sharding import PartitionSpec as P

HEADS = 16
PATCH = 4
R_DEV = 1


def shards(
    fields,
    stem_in,
    stem_out,
    level_ids,
    level_table,
    latent_query,
    kv_weight,
    out_weight,
    region_ids,
):
    nvar_local = fields.shape[0]
    rows = fields.shape[1] // PATCH
    cols = fields.shape[2] // PATCH
    width = latent_query.shape[1]
    nlatent = latent_query.shape[0]
    head_size = width // HEADS
    pixels = fields.reshape(nvar_local, rows, PATCH, cols, PATCH).transpose(0, 1, 3, 2, 4)
    pixels = pixels.reshape(nvar_local, rows, cols, PATCH * PATCH)
    stem = jax.nn.gelu(
        jnp.einsum("vabp,vpd->vabd", pixels, stem_in, preferred_element_type=jnp.float32)
    ).astype(jnp.bfloat16)
    tokens = jnp.einsum(
        "vabd,vde->vabe", stem, stem_out, preferred_element_type=jnp.float32
    ).astype(jnp.bfloat16)
    onehot = (
        level_ids[:, None] == jnp.arange(level_table.shape[0], dtype=jnp.int32)[None, :]
    ).astype(jnp.bfloat16)
    level_embed = jnp.dot(onehot, level_table, preferred_element_type=jnp.float32)
    query = latent_query.reshape(nlatent, HEADS, head_size)
    scale = 1.0 / head_size**0.5
    block = lax.all_to_all(tokens, "var", split_axis=1, concat_axis=0, tiled=True)
    nvars, arow, bcol, _ = block.shape
    keyed = block.astype(jnp.float32) + level_embed[:, None, None, :]
    centre = jnp.mean(keyed, axis=-1, keepdims=True)
    spread = jnp.mean((keyed - centre) ** 2, axis=-1, keepdims=True)
    normed = ((keyed - centre) * lax.rsqrt(spread + 1e-05)).astype(jnp.bfloat16)
    kv = jnp.einsum("vabd,de->vabe", normed, kv_weight, preferred_element_type=jnp.float32).astype(
        jnp.bfloat16
    )
    keys = kv[..., :width].reshape(nvars, arow, bcol, HEADS, head_size)
    values = kv[..., width:].reshape(nvars, arow, bcol, HEADS, head_size)
    scores = jnp.einsum("lhe,vabhe->abhlv", query, keys, preferred_element_type=jnp.float32) * scale
    weights = jax.nn.softmax(scores, axis=-1).astype(jnp.bfloat16)
    mixed = jnp.einsum(
        "abhlv,vabhe->ablhe", weights, values, preferred_element_type=jnp.float32
    ).astype(jnp.bfloat16)
    projected = jnp.dot(
        mixed.reshape(arow * bcol * nlatent, width), out_weight, preferred_element_type=jnp.float32
    )
    result = latent_query.astype(jnp.float32)[None, None] + projected.reshape(
        arow, bcol, nlatent, width
    )
    latents = result.astype(jnp.bfloat16)
    arow, bcol = (latents.shape[0], latents.shape[1])
    crow, ccol = (arow // 2, bcol // 2)
    coarse = (
        latents.astype(jnp.float32)
        .reshape(crow, 2, ccol, 2, nlatent, width)
        .mean(axis=(1, 3))
        .astype(jnp.bfloat16)
    )
    flat = coarse.reshape(crow * ccol, nlatent * width)
    first_region = lax.axis_index(("var", "band")) * R_DEV
    mine = first_region + jnp.arange(R_DEV, dtype=jnp.int32)
    all_cells = region_ids.reshape(-1)
    counts = jnp.sum((mine[:, None] == all_cells[None, :]).astype(jnp.float32), axis=1)
    nvar_axis = lax.axis_size("var")
    nband_axis = lax.axis_size("band")
    ordered = (
        region_ids.reshape(nvar_axis, crow, nband_axis, ccol).transpose(0, 2, 1, 3).reshape(-1)
    )
    select = (mine[:, None] == ordered[None, :]).astype(jnp.bfloat16)
    sums = jnp.dot(
        select,
        lax.all_gather(flat, ("var", "band"), axis=0, tiled=True),
        preferred_element_type=jnp.float32,
    )
    region_means = (sums / counts[:, None]).reshape(R_DEV, nlatent, width)
    return (latents, region_means)


def solution(mesh):
    in_specs = (
        P("var", None, "band"),
        P("var", None, None),
        P("var", None, None),
        P(),
        P(),
        P(),
        P(),
        P(),
        P(),
    )
    out_specs = (P("var", "band", None, None), P(("var", "band"), None, None))
    return jax.shard_map(shards, mesh=mesh, in_specs=in_specs, out_specs=out_specs, check_vma=False)
```

profile of v0, /device:TPU:1, one launch (start us, length us, event | category | flops | bytes accessed | tf_op | source)
XLA Modules:
  0.0 943.3 jit_solution(11763645123392205680)
XLA Ops:
  7.2 10.9 %reshape.100 = bf16[2,64,4,32,4]{4,3,2,1,0:T(8,128)(2,1)} reshape(bf16[2,256,128]{2,1,0:T(8,128)(2,1)} %param.9) | data formatting | bytes 262144 | tf_op jit(solution)/shard_map/reshape | solution.py:28
  18.1 6.1 copy.153
  24.6 6.0 fusion.22
  30.6 4.7 copy.155
  35.3 11.2 %all-to-all-start = ((bf16[2,64,32,512]{3,2,0,1:T(8,128)(2,1)}), bf16[2,64,32,512]{3,2,0,1:T(8,128)(2,1)}, u32[]{:S(2)}, u32[]{:S(2)}) async-start(bf16[2,64,32,512]{3,2,0,1:T(8,128)(2,1)} %copy.155), calls=%async_computation | async-start | bytes 8388608 | tf_op jit(solution)/shard_map/all_to_all | solution.py:42
  47.0 93.6 %all-to-all-done = bf16[2,64,32,512]{3,2,0,1:T(8,128)(2,1)} async-done(((bf16[2,64,32,512]{3,2,0,1:T(8,128)(2,1)}), bf16[2,64,32,512]{3,2,0,1:T(8,128)(2,1)}, u32[]{:S(2)}, u32[]{:S(2)}) %all-to-all-start) | async-done | bytes 4194336 | tf_op jit(solution)/shard_map/all_to_all | solution.py:42
  140.6 2.7 copy.156
  143.3 1.0 add_reduce_fusion
  144.4 1.2 convert_bitcast_fusion
  145.6 2.2 multiply_reduce_fusion
  148.1 1.9 copy.157
  149.9 1.7 fusion.11
  151.6 4.8 convolution_convert_fusion
  156.4 3.9 fusion.50
  160.3 9.2 copy.169
  169.5 4.6 fusion.12
  174.0 2.9 fusion.51
  176.9 9.2 copy.168
  186.1 8.5 fusion.30
  194.8 1.0 dot_general.32
  197.9 0.9 copy.175
  198.8 728.3 %all-gather.2.cloned.1.call-done = bf16[4096,2048]{1,0:T(8,128)(2,1)} async-done(((bf16[16,2048]{1,0:T(8,128)(2,1)}), bf16[4096,2048]{1,0:T(8,128)(2,1)}) %all-gather.2.cloned.1.call-update) | async-done | bytes 16777232 | tf_op jit(solution)/shard_map/all_gather | solution.py:86
  927.1 8.0 fusion.52
  935.2 0.7 broadcast_divide_fusion
  (42 shorter events, 4.0 us)
Async XLA Ops:
  7.2 144.5 %copy-start = (bf16[512,1024]{1,0:T(8,128)(2,1)S(1)}, bf16[512,1024]{1,0:T(8,128)(2,1)}, u32[]{:S(2)}) copy-start(bf16[512,1024]{1,0:T(8,128)(2,1)} %param.15) | copy-start | bytes 3145732
  7.2 17.4 %copy-start.8 = (bf16[2,16,512]{2,1,0:T(8,128)(2,1)S(1)}, bf16[2,16,512]{2,1,0:T(8,128)(2,1)}, u32[]{:S(2)}) copy-start(bf16[2,16,512]{2,1,0:T(8,128)(2,1)} %param.10) | copy-start | bytes 98308
  7.2 17.4 %copy-start.7 = (bf16[2,512,512]{2,1,0:T(8,128)(2,1)S(1)}, bf16[2,512,512]{2,1,0:T(8,128)(2,1)}, u32[]{:S(2)}) copy-start(bf16[2,512,512]{2,1,0:T(8,128)(2,1)} %param.11) | copy-start | bytes 3145732
  30.6 16.0 %copy-start.4 = (bf16[4,512]{1,0:T(4,128)(2,1)S(1)}, bf16[4,512]{1,0:T(4,128)(2,1)}, u32[]{:S(2)}) copy-start(bf16[4,512]{1,0:T(4,128)(2,1)} %param.14) | copy-start | bytes 12292
  30.6 16.1 %copy-start.3 = (bf16[128,512]{1,0:T(8,128)(2,1)S(1)}, bf16[128,512]{1,0:T(8,128)(2,1)}, u32[]{:S(2)}) copy-start(bf16[128,512]{1,0:T(8,128)(2,1)} %param.13) | copy-start | bytes 393220
  30.6 16.1 %copy-start.6 = (s32[64]{0:T(128)S(1)}, s32[64]{0:T(128)}, u32[]{:S(2)}) copy-start(s32[64]{0:T(128)} %param.12) | copy-start | bytes 772
  35.3 105.3 %all-to-all-start = ((bf16[2,64,32,512]{3,2,0,1:T(8,128)(2,1)}), bf16[2,64,32,512]{3,2,0,1:T(8,128)(2,1)}, u32[]{:S(2)}, u32[]{:S(2)}) async-start(bf16[2,64,32,512]{3,2,0,1:T(8,128)(2,1)} %copy.155), calls=%async_computation | async-start | bytes 8388608 | tf_op jit(solution)/shard_map/all_to_all | solution.py:42
  46.5 880.6 %all-gather.2.cloned.1.call-start = ((), (), s32[]{:S(2)}) async-start(), calls=%async_computation.1 | async-start | bytes 16842752 | tf_op jit(solution)/shard_map/all_gather | solution.py:86
  186.1 9.7 %copy-start.2 = (bf16[512,512]{1,0:T(8,128)(2,1)S(1)}, bf16[512,512]{1,0:T(8,128)(2,1)}, u32[]{:S(2)}) copy-start(bf16[512,512]{1,0:T(8,128)(2,1)} %param.16) | copy-start | bytes 1572868
  186.1 11.2 %copy-start.5 = (s32[32,128]{1,0:T(8,128)S(1)}, s32[32,128]{1,0:T(8,128)}, u32[]{:S(2)}) copy-start(s32[32,128]{1,0:T(8,128)} %param.17) | copy-start | bytes 49156
  197.9 738.5 %copy-start.1 = (bf16[512,1024]{1,0:T(8,128)(2,1)S(1)}, bf16[512,1024]{1,0:T(8,128)(2,1)}, u32[]{:S(2)}) copy-start(bf16[512,1024]{1,0:T(8,128)(2,1)} %param.15) | copy-start | bytes 3145732
Sparse Core Ops, SparseCore 0:
  197.4 729.6 all-gather.1
where the time goes:
time: 947 us; the launch traced here: 943 us
  waiting for transfers between devices  822 us (87%)
  local copies, waits for them, and re-layouts  52.8 us (6%)
  matrix products  32.4 us (3%)
  between operations  14.3 us (2%)
  starting transfers between devices  11.2 us (1%)
  other arithmetic  10.6 us (1%)
    all_gather x1, waiting for transfers between devices, shards(): lax.all_gather(flat, ('var', 'band'), axis=0, tiled=True)  728 us
    all_to_all x1, waiting for transfers between devices, shards(): lax.all_to_all(tokens, 'var', split_axis=1, concat_axis=0, tiled=True)  93.6 us
  transfers between devices with their start and end apart: 2, of which 2 were waited for; matrix products, arithmetic and copies ran while one was open for 0% of the time, Pallas kernels for 0%

commit v1 on v0

v1 whole, which is shorter than its diff:
```python
import jax
import jax.numpy as jnp
from jax import lax
from jax.experimental import pallas as pl
from jax.experimental.pallas import tpu as pltpu
from jax.sharding import PartitionSpec as P

MESH = pl.DeviceIdType.MESH
BF16 = jnp.bfloat16
F32 = jnp.float32
I32 = jnp.int32

HEADS = 16
HEAD = 32
WIDTH = 512
LATENT = 4
FLAT = LATENT * WIDTH
NZ = 8
GROUP = 4
NVAR = 32
NBAND = 8
CHUNK = 64
HALF = 32
LOG2E = 1.4426950408889634
PIECE = 128


def iota(shape, axis):
    return lax.broadcasted_iota(I32, shape, axis)


def dot(a, b):
    return jnp.dot(a, b, preferred_element_type=F32)


def dot_nt(a, b):
    return lax.dot_general(a, b, (((1,), (1,)), ((), ())), preferred_element_type=F32)


def mod(a, n):
    return lax.rem(a, jnp.int32(n))


def div(a, n):
    return lax.div(a, jnp.int32(n))


def kernel(
    fields, stem_in, stem_out, ids_hbm, table_hbm, query_hbm, kvw_hbm, outw_hbm, regions_hbm,
    lat, means,
    field_v, ids, table, query, kvw, outw, regions,
    pbuf, pown, sbuf, wbuf, fscr, lhs, tile, normed, emb, qk, ex,
    part, ms, rpart, rms, chosen, pairs, table_f, table_b, rows,
    lsem, ps, pr, ss, sr, ws, wr, xs, fs, os, orr, mss, msr, cs, cr, ts, tr,
):
    vi = lax.axis_index("var")
    bi = lax.axis_index("band")
    z = div(vi, GROUP)
    g = mod(vi, GROUP)
    ylo = div(g, 2)
    core = mod(g, 2)
    x = div(bi, 2)
    yhi = mod(bi, 2)
    y = yhi * 2 + ylo
    odd_x = mod(x, 2)
    base = z * GROUP
    g_core = ylo * 2 + 1 - core
    g_y = (1 - ylo) * 2 + core
    g_diag = (1 - ylo) * 2 + 1 - core
    core_dev = (base + g_core, bi)
    band_next = x * 2 + div(mod(y + 1, 4), 2)
    band_prev = x * 2 + div(mod(y + 3, 4), 2)
    band_far = x * 2 + 1 - yhi
    right = (vi, mod(x + 1, 4) * 2 + yhi)
    left = (vi, mod(x + 3, 4) * 2 + yhi)
    member = g * 2 + yhi
    place = z * 4 + x

    def member_dev(j):
        other = mod(member + j, 8)
        return (base + div(other, 2), x * 2 + mod(other, 2))

    def place_dev(j):
        other = mod(place + j, NVAR)
        return (div(other, 4) * GROUP + g, mod(other, 4) * 2 + yhi)

    barrier = pltpu.get_barrier_semaphore()

    def greet_member(j, carry):
        pl.semaphore_signal(barrier, inc=1, device_id=member_dev(j), device_id_type=MESH)
        return carry

    def greet_place(j, carry):
        pl.semaphore_signal(barrier, inc=1, device_id=place_dev(j), device_id_type=MESH)
        return carry

    lax.fori_loop(1, NVAR, greet_place, 0)
    lax.fori_loop(1, 8, greet_member, 0)

    local_copies = [
        pltpu.make_async_copy(src, dst, lsem.at[k])
        for k, (src, dst) in enumerate((
            (fields, field_v), (stem_out, wbuf.at[0]), (stem_in, sbuf.at[0]), (ids_hbm, ids),
            (table_hbm, table), (query_hbm, query), (kvw_hbm, kvw), (regions_hbm, regions),
            (outw_hbm, outw),
        ))
    ]
    for copy in local_copies:
        copy.start()

    local_copies[0].wait()
    ff = field_v[...].astype(F32).reshape(2, NZ, GROUP, 8, 128)
    for k in range(GROUP):
        pown[k] = ff[:, :, k].reshape(2 * NZ * 8, 128).astype(BF16)
    pbuf[0] = pown[g]

    pl.semaphore_wait(barrier, NVAR - 1 + 7)

    def piece_copy(src, s, u, j, send, target):
        start = pl.multiple_of(j * PIECE, PIECE)
        return pltpu.make_async_remote_copy(
            src_ref=src.at[u, pl.ds(start, PIECE), :], dst_ref=wbuf.at[s, u, pl.ds(start, PIECE), :],
            send_sem=send, recv_sem=wr.at[s, u, j], device_id=target, device_id_type=MESH,
        )

    def whole_copy(u, send):
        return pltpu.make_async_remote_copy(
            src_ref=stem_out.at[u], dst_ref=wbuf.at[1, u], send_sem=send,
            recv_sem=wr.at[1, u, 0], device_id=core_dev, device_id_type=MESH,
        )

    def pixel_copy(k, source, target):
        return pltpu.make_async_remote_copy(
            src_ref=pown.at[source], dst_ref=pbuf.at[k + 1], send_sem=ps.at[k],
            recv_sem=pr.at[k], device_id=target, device_id_type=MESH,
        )

    def stem_copy(k, target):
        return pltpu.make_async_remote_copy(
            src_ref=stem_in, dst_ref=sbuf.at[k + 1], send_sem=ss.at[k],
            recv_sem=sr.at[k], device_id=target, device_id_type=MESH,
        )

    next_dev = (base + g_y, band_next)
    prev_dev = (base + g_y, band_prev)
    sends = [
        pixel_copy(0, g_core, core_dev),
        stem_copy(0, core_dev),
        whole_copy(0, ws.at[4]),
        piece_copy(stem_out, 2, odd_x, 0, ws.at[0], next_dev),
        piece_copy(stem_out, 2, odd_x, 2, ws.at[2], prev_dev),
        whole_copy(1, ws.at[5]),
        pixel_copy(1, g_y, (base + g_y, bi)),
        stem_copy(1, (base + g_y, band_far)),
        piece_copy(stem_out, 2, odd_x, 1, ws.at[1], next_dev),
        piece_copy(stem_out, 2, odd_x, 3, ws.at[3], prev_dev),
        pixel_copy(2, g_diag, (base + g_diag, bi)),
        stem_copy(2, (base + g_diag, band_far)),
    ]
    for copy in sends:
        copy.start()

    def forward_x(j, target):
        return piece_copy(wbuf.at[2], 2, odd_x, j, xs.at[j], target)

    def forward_core(u, j):
        return pltpu.make_async_remote_copy(
            src_ref=wbuf.at[2, u, pl.ds(j * PIECE, PIECE), :],
            dst_ref=wbuf.at[3, u, pl.ds(j * PIECE, PIECE), :],
            send_sem=fs.at[u, j], recv_sem=wr.at[3, u, j], device_id=core_dev, device_id_type=MESH,
        )

    def arrived(s, u, j):
        piece_copy(stem_out, s, u, j, ws.at[0], core_dev).wait_recv()

    def from_y(j_right, j_left):
        arrived(2, odd_x, j_right)
        forward_x(j_right, right).start()
        forward_core(odd_x, j_right).start()
        arrived(2, odd_x, j_left)
        forward_x(j_left, left).start()
        forward_core(odd_x, j_left).start()

    def from_x(first, second):
        for j in (first, second):
            arrived(2, 1 - odd_x, j)
            forward_core(1 - odd_x, j).start()

    tile[...] = (
        (div(iota((512, 128), 0), 128) == div(iota((512, 128), 1), 4))
        & (mod(iota((512, 128), 0), 4) == mod(iota((512, 128), 1), 4))
    ).astype(F32).astype(BF16)
    for l in range(LATENT):
        lane = iota((128, 1024), 1)
        want = div(mod(lane, WIDTH), HEAD) + l * HEADS + div(lane, WIDTH) * 64
        ex[l] = (iota((128, 1024), 0) == want).astype(F32).astype(BF16)
    for copy in local_copies[3:5]:
        copy.wait()
    onehot = (iota((128, 64), 0) == ids[...]).astype(F32)
    emb[...] = dot(onehot.T.astype(BF16), table[...])
    for copy in local_copies[5:8]:
        copy.wait()
    qf = query[...].astype(F32)
    heads = iota((HEADS, WIDTH), 0) == div(iota((HEADS, WIDTH), 1), HEAD)
    qmat = jnp.concatenate(
        [jnp.where(heads, jnp.broadcast_to(qf[l:l + 1], (HEADS, WIDTH)), 0.0) for l in range(LATENT)],
        axis=0,
    ).astype(BF16)
    folded = dot_nt(qmat, kvw[:, :WIDTH]) * (LOG2E / HEAD**0.5)
    high = folded.astype(BF16).astype(F32)
    qk[...] = jnp.concatenate([high, folded - high], axis=0).T.astype(BF16)

    ones = jnp.ones((128, 128), F32)
    same_tile = div(iota((128, 128), 0), 16) == div(iota((128, 128), 1), 16)
    slot_row = iota((128, 128), 0)
    tile_lane = div(iota((128, 128), 1), 16)
    dest = iota((NVAR, 128), 0)
    dest_region = (div(dest, 4) * GROUP + g) * NBAND + mod(dest, 4) * 2 + yhi
    picked = jnp.zeros((NVAR, 128), F32)

    def slots(row):
        across = row.astype(F32) * ones
        below = jnp.where((across.T < across) & same_tile, 0.5, 0.0)
        return jnp.sum(below, axis=0, keepdims=True).astype(I32)

    for k in range(GROUP):
        row = regions[pl.ds(base + k, 1), :]
        hit = (slots(row) == mod(slot_row, 8)) & (div(slot_row, 32) == k) & (
            tile_lane == x * 2 + mod(div(slot_row, 16), 2)
        )
        in_region = (row == dest_region).astype(F32).astype(BF16)
        picked = picked + dot_nt(in_region, jnp.where(hit, 0.5, 0.0).astype(BF16))
    upper = mod(div(iota((NVAR, 128), 1), 8), 2) == 1
    chosen[...] = jnp.concatenate(
        [jnp.where(upper, 0.0, picked), jnp.where(upper, picked, 0.0)], axis=0
    ).astype(BF16)
    own_row = regions[pl.ds(vi, 1), :]
    own_hit = (slots(own_row) == iota((8, 128), 0)) & (div(iota((8, 128), 1), 16) == bi)
    cell = div(mod(iota((128, CHUNK), 1), HALF), 2)
    average = jnp.where(mod(iota((128, CHUNK), 0), 16) == cell, 0.25, 0.0).astype(BF16)
    pair_mean = dot(own_hit.astype(F32).astype(BF16), average).astype(BF16)
    region = vi * NBAND + bi
    count = jnp.sum((regions[...] == region).astype(F32))

    local_copies[1].wait()
    local_copies[2].wait()
    patch_mask = div(iota((HALF, 128), 1), 4) == iota((HALF, 128), 0)

    def one_variable(t, carry):
        late = div(t, 4)
        s = (1 - late) * div(t, 2) + late * (2 + mod(t, 2))
        second = div(t, 6)
        u = (1 - late) * mod(t, 2) + late * (odd_x + second - 2 * odd_x * second)

        @pl.when(t == 2)
        def _():
            pixel_copy(0, 0, core_dev).wait_recv()
            stem_copy(0, core_dev).wait_recv()
            whole_copy(0, ws.at[4]).wait_recv()

        @pl.when(t == 3)
        def _():
            from_y(0, 2)
            whole_copy(1, ws.at[5]).wait_recv()

        @pl.when(t == 4)
        def _():
            from_y(3, 1)
            pixel_copy(1, 0, core_dev).wait_recv()
            stem_copy(1, core_dev).wait_recv()

        @pl.when(t == 5)
        def _():
            from_x(0, 2)
            pixel_copy(2, 0, core_dev).wait_recv()
            stem_copy(2, core_dev).wait_recv()

        @pl.when(t == 6)
        def _():
            from_x(3, 1)

        @pl.when((t == 5) | (t == 7))
        def _():
            for j in range(4):
                arrived(3, u, j)

        fscr[...] = pbuf[s, pl.ds(pl.multiple_of(u * CHUNK, CHUNK), CHUNK), :].astype(F32)
        for a in range(16):
            for i in range(4):
                row = jnp.broadcast_to(fscr[pl.ds(a * 4 + i, 1), :], (HALF, 128))
                lhs[pl.ds(a * HALF, HALF), pl.ds(i * 128, 128)] = jnp.where(
                    patch_mask, row, 0.0
                ).astype(BF16)
        pixels = dot(lhs[...], tile[...]).astype(BF16)[:, :16]
        x = dot(pixels, sbuf[s, u])
        stem = (0.5 * x * (1.0 + jnp.tanh(0.7978845608028654 * (x + 0.044715 * (x * x * x))))).astype(BF16)
        tokens = dot(stem, wbuf[s, u]).astype(BF16).astype(F32)
        src_g = mod(s, 2)
        src_core = core + src_g - 2 * core * src_g
        up = div(s, 2)
        src_y = ylo + up - 2 * ylo * up
        var = (base + src_y * 2 + src_core) * 2 + u
        keyed = tokens + emb[pl.ds(var, 1), :]
        centre = jnp.mean(keyed, axis=-1, keepdims=True)
        away = keyed - centre
        spread = jnp.mean(away * away, axis=-1, keepdims=True)
        normed[t] = (away * lax.rsqrt(spread + 1e-05)).astype(BF16)
        return carry

    lax.fori_loop(0, 8, one_variable, 0)

    low_lanes = iota((CHUNK, 128), 1) < 64

    def ring_copies(dr, d, half):
        off = mod(d + dr * (8 - 2 * d), 8)
        target = (mod(z + 1 + 6 * dr, NZ) * GROUP + g, bi)
        start = pl.multiple_of(half * HALF, HALF)
        return (
            pltpu.make_async_remote_copy(
                src_ref=ms.at[off, pl.ds(start, HALF), :], dst_ref=rms.at[dr, d - 1, half],
                send_sem=mss.at[dr, d - 1, half], recv_sem=msr.at[dr, d - 1, half],
                device_id=target, device_id_type=MESH,
            ),
            pltpu.make_async_remote_copy(
                src_ref=part.at[off, pl.ds(start, HALF), :], dst_ref=rpart.at[dr, d - 1, half],
                send_sem=os.at[dr, d - 1, half], recv_sem=orr.at[dr, d - 1, half],
                device_id=target, device_id_type=MESH,
            ),
        )

    def ring_send(dr, d, half):
        for copy in ring_copies(dr, d, half):
            copy.start()

    def local(off):
        start = pl.multiple_of(mod(z + off, NZ) * CHUNK, CHUNK)
        nb = normed[:, pl.ds(start, CHUNK), :].reshape(8 * CHUNK, WIDTH)
        scores = dot(nb, qk[...])
        scores = (scores + pltpu.roll(scores, 64, 1)).reshape(8, CHUNK, 128)
        top = jnp.ceil(jnp.max(scores, axis=0))
        p = jnp.exp2(scores - top[None])
        ms[off] = jnp.where(low_lanes, top, jnp.sum(p, axis=0))
        pb = p.astype(BF16).reshape(8 * CHUNK, 128)
        values = dot(nb, kvw[:, WIDTH:])
        for l in range(LATENT):
            wide = dot(pb, ex[l, :, :WIDTH])
            part[off, :, l * WIDTH:(l + 1) * WIDTH] = jnp.sum(
                (wide * values).reshape(8, CHUNK, WIDTH), axis=0
            ).astype(BF16)

    def offset(dr, d):
        return mod(d + dr * (8 - 2 * d), 8)

    def merge(d, half):
        parts = []
        for dr, h in ((0, half), (1, 1 - half)):
            parts.append((dr, h, offset(dr, d), pl.ds(pl.multiple_of(h * HALF, HALF), HALF)))
        mine = jnp.concatenate([ms[off, at, :] for _, _, off, at in parts], axis=0)
        other = jnp.concatenate([rms[dr, d, h] for dr, h, _, _ in parts], axis=0)
        mine_r = pltpu.roll(mine, 64, 1)
        other_r = pltpu.roll(other, 64, 1)
        m1 = jnp.where(low_lanes, mine, mine_r)
        s1 = jnp.where(low_lanes, mine_r, mine)
        m2 = jnp.where(low_lanes, other, other_r)
        s2 = jnp.where(low_lanes, other_r, other)
        m = jnp.maximum(m1, m2)
        a1 = jnp.exp2(m1 - m)
        a2 = jnp.exp2(m2 - m)
        new = jnp.where(low_lanes, m, a1 * s1 + a2 * s2)
        ab = jnp.where(low_lanes, a2, a1).astype(BF16)
        for k, (_, _, off, at) in enumerate(parts):
            ms[off, at, :] = new[k * HALF:(k + 1) * HALF]
        for l in range(LATENT):
            cols = slice(l * WIDTH, (l + 1) * WIDTH)
            factor = dot(ab, ex[l])
            for k, (dr, h, off, at) in enumerate(parts):
                lines = slice(k * HALF, (k + 1) * HALF)
                part[off, at, cols] = (
                    factor[lines, :WIDTH] * rpart[dr, d, h, :, cols].astype(F32)
                    + factor[lines, WIDTH:] * part[off, at, cols].astype(F32)
                ).astype(BF16)

    def merge_step(d):
        def one(i, carry):
            half = 1 - i

            @pl.when((d < 3) | (i > 0))
            def _():
                for dr, h in ((0, half), (1, i)):
                    for copy in ring_copies(dr, d + 1, h):
                        copy.wait_recv()
                merge(d, half)

            @pl.when(d > 0)
            def _():
                ring_send(0, d, half)
                ring_send(1, d, i)

            return carry

        lax.fori_loop(0, 2, one, 0)

    def one_chunk(k, carry):
        odd = mod(k, 2)
        local(4 - div(k + 1, 2) * odd + div(k, 2) * (1 - odd))

        @pl.when(k == 0)
        def _():
            ring_send(0, 4, 0)
            ring_send(1, 4, 1)

        @pl.when((odd == 0) & (k > 0))
        def _():
            merge_step(4 - div(k, 2))

        return carry

    lax.fori_loop(0, 7, one_chunk, 0)
    local(0)
    merge_step(0)

    total = ms[0]
    inverse = 1.0 / jnp.where(low_lanes, pltpu.roll(total, 64, 1), total)
    inv_high = inverse.astype(BF16).astype(F32)
    inv = jnp.where(low_lanes, inv_high, inverse - inv_high).astype(BF16)
    mixed = []
    for l in range(LATENT):
        factor = dot(inv, ex[l])
        mixed.append(
            (part[0, :, l * WIDTH:(l + 1) * WIDTH].astype(F32)
             * (factor[:, :WIDTH] + factor[:, WIDTH:])).astype(BF16)
        )
    local_copies[8].wait()
    projected = dot(jnp.concatenate(mixed, axis=0), outw[...])
    sums = []
    for l in range(LATENT):
        cols = slice(l * WIDTH, (l + 1) * WIDTH)
        out = (projected[l * CHUNK:(l + 1) * CHUNK] + qf[l:l + 1]).astype(BF16)
        lat[:, cols] = out
        sums.append(dot(pair_mean, out))
    pairs[member] = jnp.concatenate(
        [jnp.concatenate(sums[:2], axis=1), jnp.concatenate(sums[2:], axis=1)], axis=0
    ).astype(BF16)

    def pair_copy(j, slot):
        return pltpu.make_async_remote_copy(
            src_ref=pairs.at[slot], dst_ref=pairs.at[slot], send_sem=cs.at[j], recv_sem=cr.at[j],
            device_id=member_dev(j), device_id_type=MESH,
        )

    def pair_send(j, carry):
        pair_copy(j, member).start()
        return carry

    def pair_wait(j, carry):
        pair_copy(j, mod(member + 8 - j, 8)).wait_recv()
        return carry

    lax.fori_loop(1, 8, pair_send, 0)
    lax.fori_loop(1, 8, pair_wait, 0)
    by_dest = dot(chosen[...], pairs[...].reshape(128, 2 * WIDTH))
    for k in range(16):
        table_f[:, k, :] = by_dest[(k // 8) * NVAR:(k // 8 + 1) * NVAR, (k % 8) * 128:(k % 8 + 1) * 128]
    table_b[...] = table_f[...].astype(BF16)

    def row_copy(j):
        return pltpu.make_async_remote_copy(
            src_ref=table_b.at[mod(place + j, NVAR)], dst_ref=rows.at[j], send_sem=ts.at[j],
            recv_sem=tr.at[j], device_id=place_dev(j), device_id_type=MESH,
        )

    def row_send(j, carry):
        row_copy(j).start()
        return carry

    def row_wait(j, carry):
        row_copy(j).wait_recv()
        return carry

    lax.fori_loop(1, NVAR, row_send, 0)
    rows[0] = table_b[place]
    lax.fori_loop(1, NVAR, row_wait, 0)
    total = jnp.sum(rows[...].astype(F32), axis=0) / count
    for l in range(LATENT):
        for k in range(4):
            means[0, l:l + 1, k * 128:(k + 1) * 128] = total[l * 4 + k:l * 4 + k + 1, :]

    for copy in sends:
        copy.wait_send()
    for j in range(4):
        forward_x(j, right).wait_send()
        forward_core(0, j).wait_send()
        forward_core(1, j).wait_send()

    def ring_over(i, carry):
        dr = mod(i, 2)
        half = mod(div(i, 2), 2)
        d = 1 + div(i, 4)

        @pl.when((d < 4) | (half == dr))
        def _():
            for copy in ring_copies(dr, d, half):
                copy.wait_send()

        return carry

    def pair_over(j, carry):
        pair_copy(j, member).wait_send()
        return carry

    def row_over(j, carry):
        row_copy(j).wait_send()
        return carry

    lax.fori_loop(0, 16, ring_over, 0)
    lax.fori_loop(1, 8, pair_over, 0)
    lax.fori_loop(1, NVAR, row_over, 0)


def shards(fields, stem_in, stem_out, level_ids, level_table, latent_query, kv_weight, out_weight, region_ids):
    vmem = pl.BlockSpec(memory_space=pltpu.VMEM)
    dma = pltpu.SemaphoreType.DMA
    lat, means = pl.pallas_call(
        kernel,
        out_shape=(
            jax.ShapeDtypeStruct((CHUNK, FLAT), BF16),
            jax.ShapeDtypeStruct((1, LATENT, WIDTH), F32),
        ),
        in_specs=[pl.BlockSpec(memory_space=pl.ANY)] * 9,
        out_specs=(vmem, vmem),
        scratch_shapes=[
            pltpu.VMEM((2, 256, 128), BF16),
            pltpu.VMEM((1, 64), I32),
            pltpu.VMEM((128, WIDTH), BF16),
            pltpu.VMEM((LATENT, WIDTH), BF16),
            pltpu.VMEM((WIDTH, 2 * WIDTH), BF16),
            pltpu.VMEM((WIDTH, WIDTH), BF16),
            pltpu.VMEM((32, 128), I32),
            pltpu.VMEM((GROUP, 128, 128), BF16),
            pltpu.VMEM((GROUP, 128, 128), BF16),
            pltpu.VMEM((GROUP, 2, 16, WIDTH), BF16),
            pltpu.VMEM((GROUP, 2, WIDTH, WIDTH), BF16),
            pltpu.VMEM((CHUNK, 128), F32),
            pltpu.VMEM((512, 512), BF16),
            pltpu.VMEM((512, 128), BF16),
            pltpu.VMEM((8, 512, WIDTH), BF16),
            pltpu.VMEM((64, WIDTH), F32),
            pltpu.VMEM((WIDTH, 128), BF16),
            pltpu.VMEM((LATENT, 128, 2 * WIDTH), BF16),
            pltpu.VMEM((NZ, CHUNK, FLAT), BF16),
            pltpu.VMEM((NZ, CHUNK, 128), F32),
            pltpu.VMEM((2, 4, 2, HALF, FLAT), BF16),
            pltpu.VMEM((2, 4, 2, HALF, 128), F32),
            pltpu.VMEM((2 * NVAR, 128), BF16),
            pltpu.VMEM((8, 16, 2 * WIDTH), BF16),
            pltpu.VMEM((NVAR, 16, 128), F32),
            pltpu.VMEM((NVAR, 16, 128), BF16),
            pltpu.VMEM((NVAR, 16, 128), BF16),
            dma((9,)),
            dma((3,)), dma((3,)),
            dma((3,)), dma((3,)),
            dma((6,)), dma((GROUP, 2, 4)), dma((4,)), dma((2, 4)),
            dma((2, 4, 2)), dma((2, 4, 2)),
            dma((2, 4, 2)), dma((2, 4, 2)),
            dma((8,)), dma((8,)),
            dma((NVAR,)), dma((NVAR,)),
        ],
        compiler_params=pltpu.CompilerParams(
            collective_id=0, has_side_effects=True, vmem_limit_bytes=60 * 1024 * 1024
        ),
        name="window",
    )(
        fields, stem_in, stem_out, level_ids.reshape(1, -1), level_table, latent_query,
        kv_weight, out_weight, region_ids,
    )
    return lat.reshape(2, 32, LATENT, WIDTH), means


def solution(mesh):
    in_specs = (
        P("var", None, "band"),
        P("var", None, None),
        P("var", None, None),
        P(),
        P(),
        P(),
        P(),
        P(),
        P(),
    )
    out_specs = (P("var", "band", None, None), P(("var", "band"), None, None))
    return jax.shard_map(shards, mesh=mesh, in_specs=in_specs, out_specs=out_specs, check_vma=False)
```

time: 947 us -> 72.5 us (0.08)
  waiting for transfers between devices: 822 us -> 0 us
  Pallas kernels: 0 us -> 68.6 us
  local copies, waits for them, and re-layouts: 52.8 us -> 2.44 us
  matrix products: 32.4 us -> 0 us
  between operations: 14.3 us -> 0.65 us
  starting transfers between devices: 11.2 us -> 0 us
  other arithmetic: 10.6 us -> 0 us
    all_gather x1 -> x0, waiting for transfers between devices: 728 us -> none  [shards(): lax.all_gather(flat, ('var', 'band'), axis=0, tiled=True)]
    all_to_all x1 -> x0, waiting for transfers between devices: 93.6 us -> none  [shards(): lax.all_to_all(tokens, 'var', split_axis=1, concat_axis=0, tiled=True)]
    pallas_call x0 -> x1, Pallas kernels: none -> 68.6 us  [shards(): pl.pallas_call(kernel, out_shape=(jax.ShapeDtypeStruct((CHUNK, FLAT), BF1...]
    dot_general x7 -> x0, matrix products: 32.4 us -> none  [the longest x1 8.54 us: shards(): jnp.einsum('abhlv,vabhe->ablhe', weights, values, preferred_element_type=...]
    slice x3 -> x0, local copies, waits for them, and re-layouts: 22.2 us -> none  [the longest x2 13.1 us: shards(): keys = kv[..., :width].reshape(nvars, arow, bcol, HEADS, head_size)]
    all_to_all x1 -> x0, starting transfers between devices: 11.2 us -> none  [shards(): lax.all_to_all(tokens, 'var', split_axis=1, concat_axis=0, tiled=True)]
    reshape x4 -> x1, local copies, waits for them, and re-layouts: 12 us -> 1.84 us  [shards(): return (lat.reshape(2, 32, LATENT, WIDTH), means)]
  transfers between devices with their start and end apart: 2 -> 0, of which waited for: 2 -> 0; matrix products, arithmetic and copies ran while one was open for 0% -> 0% of each run, Pallas kernels for 0% -> 0%
where the time goes in v1:
time: 72.5 us; the launch traced here: 71.7 us
  Pallas kernels  68.6 us (95%)
  local copies, waits for them, and re-layouts  2.44 us (3%)
    pallas_call x1, Pallas kernels, shards(): pl.pallas_call(kernel, out_shape=(jax.ShapeDtypeStruct((CHUNK, FLAT), BF1...  68.6 us
    reshape x1, local copies, waits for them, and re-layouts, shards(): return (lat.reshape(2, 32, LATENT, WIDTH), means)  1.84 us

profile of v1, /device:TPU:1, one launch (start us, length us, event | category | flops | bytes accessed | tf_op | source)
XLA Modules:
  0.0 71.7 jit_solution(8806247634672000946)
XLA Ops:
  0.6 68.6 %window.1 = (bf16[64,2048]{1,0:T(8,128)(2,1)}, f32[1,4,512]{2,1,0:T(4,128)}) custom-call(bf16[2,256,128]{2,1,0:T(8,128)(2,1)} %fields.1, bf16[2,16,512]{2,1,0:T(8,128)(2,1)} %stem_in.1, bf16[2,512,512]{2,1,0:T(8,128)(2,1)} %stem_out.1, s32[1,64]{1,0:T(1,128)} %bitcast.1, bf16[128,512]{1,0:T(8,128)(2,1)} %table_hbm.1, bf16[4,512]{1,0:T(4,128)(2,1)} %query_hbm.1, ...), custom_call_target="tpu_custom_call" | custom-call | tf_op jit(solution)/shard_map/window/pallas_call | solution.py:523
  69.2 0.0 copy-start
  69.2 1.8 %reshape.11 = bf16[2,32,4,512]{3,2,1,0:T(4,128)(2,1)} reshape(bf16[64,2048]{1,0:T(8,128)(2,1)} %get-tuple-element.4) | data formatting | bytes 524288 | tf_op jit(solution)/shard_map/reshape | solution.py:576
  71.1 0.0 copy-done
  71.1 0.6 copy.12
Async XLA Ops:
  69.2 1.9 %copy-start = (f32[1,4,512]{2,1,0:T(4,128)S(1)}, f32[1,4,512]{2,1,0:T(4,128)}, u32[]{:S(2)}) copy-start(f32[1,4,512]{2,1,0:T(4,128)} %get-tuple-element.9) | copy-start | bytes 24580

commit v2 on v1

--- a/solution.py
+++ b/solution.py
@@ -22,7 +22,7 @@
 CHUNK = 64
 HALF = 32
 LOG2E = 1.4426950408889634
-PIECE = 128
+PIECES = ((0, 128), (128, 128), (256, 64), (320, 64), (384, 64), (448, 64))
 
 
 def iota(shape, axis):
@@ -74,28 +74,26 @@
     right = (vi, mod(x + 1, 4) * 2 + yhi)
     left = (vi, mod(x + 3, 4) * 2 + yhi)
     member = g * 2 + yhi
-    place = z * 4 + x
+
+    def flip(bit, by):
+        return mod(bit + by, 2)
 
     def member_dev(j):
-        other = mod(member + j, 8)
-        return (base + div(other, 2), x * 2 + mod(other, 2))
-
-    def place_dev(j):
-        other = mod(place + j, NVAR)
-        return (div(other, 4) * GROUP + g, mod(other, 4) * 2 + yhi)
+        other = flip(ylo, j // 4) * 2 + flip(core, (j // 2) % 2)
+        return (base + other, x * 2 + flip(yhi, j % 2))
+
+    def place_off(i):
+        a, b = div(i, 4), mod(i, 4)
+        da = 4 - div(a + 1, 2) * mod(a, 2) + div(a, 2) * (1 - mod(a, 2))
+        db = 2 - div(b + 1, 2) * mod(b, 2) + div(b, 2) * (1 - mod(b, 2))
+        return mod(z + da, NZ), mod(x + db, 4)
 
     barrier = pltpu.get_barrier_semaphore()
-
-    def greet_member(j, carry):
-        pl.semaphore_signal(barrier, inc=1, device_id=member_dev(j), device_id_type=MESH)
-        return carry
-
-    def greet_place(j, carry):
-        pl.semaphore_signal(barrier, inc=1, device_id=place_dev(j), device_id_type=MESH)
-        return carry
-
-    lax.fori_loop(1, NVAR, greet_place, 0)
-    lax.fori_loop(1, 8, greet_member, 0)
+    near = [member_dev(j) for j in range(1, 8)]
+    near += [(vi, mod(x + j, 4) * 2 + yhi) for j in range(1, 4)]
+    near += [(mod(z + j, NZ) * GROUP + g, bi) for j in (1, NZ - 1)]
+    for device in near:
+        pl.semaphore_signal(barrier, inc=1, device_id=device, device_id_type=MESH)
 
     local_copies = [
         pltpu.make_async_copy(src, dst, lsem.at[k])
@@ -108,83 +106,82 @@
     for copy in local_copies:
         copy.start()
 
+    pl.semaphore_wait(barrier, len(near))
+
+    def piece_copy(src, s, u, j, send, target):
+        at = pl.ds(*PIECES[j])
+        return pltpu.make_async_remote_copy(
+            src_ref=src.at[u, at, :], dst_ref=wbuf.at[s, u, at, :],
+            send_sem=send, recv_sem=wr.at[s, u, j], device_id=target, device_id_type=MESH,
+        )
+
+    def whole_copy(u, send):
+        return pltpu.make_async_remote_copy(
+            src_ref=stem_out.at[u], dst_ref=wbuf.at[1, u], send_sem=send,
+            recv_sem=wr.at[1, u, 0], device_id=core_dev, device_id_type=MESH,
+        )
+
+    def pixel_copy(k, source, target):
+        return pltpu.make_async_remote_copy(
+            src_ref=pown.at[source], dst_ref=pbuf.at[k + 1], send_sem=ps.at[k],
+            recv_sem=pr.at[k], device_id=target, device_id_type=MESH,
+        )
+
+    def stem_copy(k, target):
+        return pltpu.make_async_remote_copy(
+            src_ref=stem_in, dst_ref=sbuf.at[k + 1], send_sem=ss.at[k],
+            recv_sem=sr.at[k], device_id=target, device_id_type=MESH,
+        )
+
+    next_dev = (base + g_y, band_next)
+    prev_dev = (base + g_y, band_prev)
+    sends = [
+        piece_copy(stem_out, 2, odd_x, 0, ws.at[0], next_dev),
+        piece_copy(stem_out, 2, odd_x, 1, ws.at[1], prev_dev),
+        piece_copy(stem_out, 2, odd_x, 2, ws.at[2], next_dev),
+        piece_copy(stem_out, 2, odd_x, 3, ws.at[3], prev_dev),
+        whole_copy(0, ws.at[10]),
+        stem_copy(0, core_dev),
+        stem_copy(1, (base + g_y, band_far)),
+        stem_copy(2, (base + g_diag, band_far)),
+        whole_copy(1, ws.at[11]),
+    ]
+    later = [
+        pixel_copy(0, g_core, core_dev),
+        pixel_copy(1, g_y, (base + g_y, bi)),
+        pixel_copy(2, g_diag, (base + g_diag, bi)),
+        piece_copy(stem_out, 2, odd_x, 4, ws.at[4], next_dev),
+        piece_copy(stem_out, 2, odd_x, 5, ws.at[5], prev_dev),
+        piece_copy(stem_out, 2, 1 - odd_x, 4, ws.at[6], next_dev),
+        piece_copy(stem_out, 2, 1 - odd_x, 5, ws.at[7], prev_dev),
+    ]
+    for copy in sends:
+        copy.start()
     local_copies[0].wait()
     ff = field_v[...].astype(F32).reshape(2, NZ, GROUP, 8, 128)
     for k in range(GROUP):
         pown[k] = ff[:, :, k].reshape(2 * NZ * 8, 128).astype(BF16)
+    for copy in later:
+        copy.start()
+    sends = sends + later
     pbuf[0] = pown[g]
-
-    pl.semaphore_wait(barrier, NVAR - 1 + 7)
-
-    def piece_copy(src, s, u, j, send, target):
-        start = pl.multiple_of(j * PIECE, PIECE)
-        return pltpu.make_async_remote_copy(
-            src_ref=src.at[u, pl.ds(start, PIECE), :], dst_ref=wbuf.at[s, u, pl.ds(start, PIECE), :],
-            send_sem=send, recv_sem=wr.at[s, u, j], device_id=target, device_id_type=MESH,
-        )
-
-    def whole_copy(u, send):
-        return pltpu.make_async_remote_copy(
-            src_ref=stem_out.at[u], dst_ref=wbuf.at[1, u], send_sem=send,
-            recv_sem=wr.at[1, u, 0], device_id=core_dev, device_id_type=MESH,
-        )
-
-    def pixel_copy(k, source, target):
-        return pltpu.make_async_remote_copy(
-            src_ref=pown.at[source], dst_ref=pbuf.at[k + 1], send_sem=ps.at[k],
-            recv_sem=pr.at[k], device_id=target, device_id_type=MESH,
-        )
-
-    def stem_copy(k, target):
-        return pltpu.make_async_remote_copy(
-            src_ref=stem_in, dst_ref=sbuf.at[k + 1], send_sem=ss.at[k],
-            recv_sem=sr.at[k], device_id=target, device_id_type=MESH,
-        )
-
-    next_dev = (base + g_y, band_next)
-    prev_dev = (base + g_y, band_prev)
-    sends = [
-        pixel_copy(0, g_core, core_dev),
-        stem_copy(0, core_dev),
-        whole_copy(0, ws.at[4]),
-        piece_copy(stem_out, 2, odd_x, 0, ws.at[0], next_dev),
-        piece_copy(stem_out, 2, odd_x, 2, ws.at[2], prev_dev),
-        whole_copy(1, ws.at[5]),
-        pixel_copy(1, g_y, (base + g_y, bi)),
-        stem_copy(1, (base + g_y, band_far)),
-        piece_copy(stem_out, 2, odd_x, 1, ws.at[1], next_dev),
-        piece_copy(stem_out, 2, odd_x, 3, ws.at[3], prev_dev),
-        pixel_copy(2, g_diag, (base + g_diag, bi)),
-        stem_copy(2, (base + g_diag, band_far)),
-    ]
-    for copy in sends:
-        copy.start()
 
     def forward_x(j, target):
         return piece_copy(wbuf.at[2], 2, odd_x, j, xs.at[j], target)
 
     def forward_core(u, j):
+        at = pl.ds(*PIECES[j])
         return pltpu.make_async_remote_copy(
-            src_ref=wbuf.at[2, u, pl.ds(j * PIECE, PIECE), :],
-            dst_ref=wbuf.at[3, u, pl.ds(j * PIECE, PIECE), :],
+            src_ref=wbuf.at[2, u, at, :], dst_ref=wbuf.at[3, u, at, :],
             send_sem=fs.at[u, j], recv_sem=wr.at[3, u, j], device_id=core_dev, device_id_type=MESH,
         )
 
     def arrived(s, u, j):
         piece_copy(stem_out, s, u, j, ws.at[0], core_dev).wait_recv()
 
-    def from_y(j_right, j_left):
-        arrived(2, odd_x, j_right)
-        forward_x(j_right, right).start()
-        forward_core(odd_x, j_right).start()
-        arrived(2, odd_x, j_left)
-        forward_x(j_left, left).start()
-        forward_core(odd_x, j_left).start()
-
-    def from_x(first, second):
-        for j in (first, second):
-            arrived(2, 1 - odd_x, j)
-            forward_core(1 - odd_x, j).start()
+    def take_rest(u, pieces):
+        for j in pieces:
+            forward_core(u, j).start()
 
     tile[...] = (
         (div(iota((512, 128), 0), 128) == div(iota((512, 128), 1), 4))
@@ -246,43 +243,21 @@
     local_copies[2].wait()
     patch_mask = div(iota((HALF, 128), 1), 4) == iota((HALF, 128), 0)
 
-    def one_variable(t, carry):
+    def which(t):
         late = div(t, 4)
-        s = (1 - late) * div(t, 2) + late * (2 + mod(t, 2))
         second = div(t, 6)
-        u = (1 - late) * mod(t, 2) + late * (odd_x + second - 2 * odd_x * second)
-
-        @pl.when(t == 2)
-        def _():
-            pixel_copy(0, 0, core_dev).wait_recv()
-            stem_copy(0, core_dev).wait_recv()
-            whole_copy(0, ws.at[4]).wait_recv()
-
-        @pl.when(t == 3)
-        def _():
-            from_y(0, 2)
-            whole_copy(1, ws.at[5]).wait_recv()
-
-        @pl.when(t == 4)
-        def _():
-            from_y(3, 1)
-            pixel_copy(1, 0, core_dev).wait_recv()
-            stem_copy(1, core_dev).wait_recv()
-
-        @pl.when(t == 5)
-        def _():
-            from_x(0, 2)
-            pixel_copy(2, 0, core_dev).wait_recv()
-            stem_copy(2, core_dev).wait_recv()
-
-        @pl.when(t == 6)
-        def _():
-            from_x(3, 1)
-
-        @pl.when((t == 5) | (t == 7))
-        def _():
-            for j in range(4):
-                arrived(3, u, j)
+        return (
+            (1 - late) * div(t, 2) + late * (2 + mod(t, 2)),
+            (1 - late) * mod(t, 2) + late * (odd_x + second - 2 * odd_x * second),
+        )
+
+    def first_matrix(t):
+        s, u = which(t)
+        for k in range(3):
+            @pl.when(t == (2, 4, 5)[k])
+            def _():
+                pixel_copy(k, 0, core_dev).wait_recv()
+                stem_copy(k, core_dev).wait_recv()
 
         fscr[...] = pbuf[s, pl.ds(pl.multiple_of(u * CHUNK, CHUNK), CHUNK), :].astype(F32)
         for a in range(16):
@@ -292,9 +267,43 @@
                     patch_mask, row, 0.0
                 ).astype(BF16)
         pixels = dot(lhs[...], tile[...]).astype(BF16)[:, :16]
-        x = dot(pixels, sbuf[s, u])
-        stem = (0.5 * x * (1.0 + jnp.tanh(0.7978845608028654 * (x + 0.044715 * (x * x * x))))).astype(BF16)
-        tokens = dot(stem, wbuf[s, u]).astype(BF16).astype(F32)
+        h = dot(pixels, sbuf[s, u])
+        stem = 0.5 * h * (1.0 + jnp.tanh(0.7978845608028654 * (h + 0.044715 * (h * h * h))))
+        normed[t] = stem.astype(BF16)
+
+    def second_matrix(t):
+        s, u = which(t)
+
+        @pl.when(t == 2)
+        def _():
+            whole_copy(0, ws.at[0]).wait_recv()
+
+        @pl.when(t == 3)
+        def _():
+            for j in range(4):
+                arrived(2, odd_x, j)
+                forward_x(j, (right, left)[j % 2]).start()
+            take_rest(odd_x, range(4))
+            whole_copy(1, ws.at[0]).wait_recv()
+
+        @pl.when(t == 4)
+        def _():
+            for j in (4, 5):
+                arrived(2, odd_x, j)
+            take_rest(odd_x, (4, 5))
+
+        @pl.when(t == 6)
+        def _():
+            for j in range(6):
+                arrived(2, 1 - odd_x, j)
+                forward_core(1 - odd_x, j).start()
+
+        @pl.when((t == 5) | (t == 7))
+        def _():
+            for j in range(6):
+                arrived(3, u, j)
+
+        tokens = dot(normed[t], wbuf[s, u]).astype(BF16).astype(F32)
         src_g = mod(s, 2)
         src_core = core + src_g - 2 * core * src_g
         up = div(s, 2)
@@ -305,9 +314,19 @@
         away = keyed - centre
         spread = jnp.mean(away * away, axis=-1, keepdims=True)
         normed[t] = (away * lax.rsqrt(spread + 1e-05)).astype(BF16)
+
+    def one_variable(t, carry):
+        @pl.when(t < 8)
+        def _():
+            first_matrix(t)
+
+        @pl.when(t > 0)
+        def _():
+            second_matrix(t - 1)
+
         return carry
 
-    lax.fori_loop(0, 8, one_variable, 0)
+    lax.fori_loop(0, 9, one_variable, 0)
 
     low_lanes = iota((CHUNK, 128), 1) < 64
 
@@ -351,9 +370,12 @@
     def offset(dr, d):
         return mod(d + dr * (8 - 2 * d), 8)
 
-    def merge(d, half):
+    def incoming(d, i):
+        for dr, h in ((0, 1 - i), (1, i)):
+            for copy in ring_copies(dr, d + 1, h):
+                copy.wait_recv()
         parts = []
-        for dr, h in ((0, half), (1, 1 - half)):
+        for dr, h in ((0, 1 - i), (1, i)):
             parts.append((dr, h, offset(dr, d), pl.ds(pl.multiple_of(h * HALF, HALF), HALF)))
         mine = jnp.concatenate([ms[off, at, :] for _, _, off, at in parts], axis=0)
         other = jnp.concatenate([rms[dr, d, h] for dr, h, _, _ in parts], axis=0)
@@ -366,7 +388,11 @@
         m = jnp.maximum(m1, m2)
         a1 = jnp.exp2(m1 - m)
         a2 = jnp.exp2(m2 - m)
-        new = jnp.where(low_lanes, m, a1 * s1 + a2 * s2)
+        return parts, m, a1, a2, a1 * s1 + a2 * s2
+
+    def merge(d, i):
+        parts, m, a1, a2, s = incoming(d, i)
+        new = jnp.where(low_lanes, m, s)
         ab = jnp.where(low_lanes, a2, a1).astype(BF16)
         for k, (_, _, off, at) in enumerate(parts):
             ms[off, at, :] = new[k * HALF:(k + 1) * HALF]
@@ -380,55 +406,46 @@
                     + factor[lines, WIDTH:] * part[off, at, cols].astype(F32)
                 ).astype(BF16)
 
-    def merge_step(d):
-        def one(i, carry):
-            half = 1 - i
-
-            @pl.when((d < 3) | (i > 0))
-            def _():
-                for dr, h in ((0, half), (1, i)):
-                    for copy in ring_copies(dr, d + 1, h):
-                        copy.wait_recv()
-                merge(d, half)
-
-            @pl.when(d > 0)
-            def _():
-                ring_send(0, d, half)
-                ring_send(1, d, i)
-
-            return carry
-
-        lax.fori_loop(0, 2, one, 0)
-
     def one_chunk(k, carry):
         odd = mod(k, 2)
-        local(4 - div(k + 1, 2) * odd + div(k, 2) * (1 - odd))
+        d = 3 - div(k - 2, 2)
+        i = mod(k, 2)
+
+        @pl.when(k < 8)
+        def _():
+            local(4 - div(k + 1, 2) * odd + div(k, 2) * (1 - odd))
 
         @pl.when(k == 0)
         def _():
             ring_send(0, 4, 0)
             ring_send(1, 4, 1)
 
-        @pl.when((odd == 0) & (k > 0))
-        def _():
-            merge_step(4 - div(k, 2))
+        @pl.when(k > 2)
+        def _():
+            merge(d, i)
+
+        @pl.when((k > 1) & (k < 8))
+        def _():
+            ring_send(0, d, 1 - i)
+            ring_send(1, d, i)
 
         return carry
 
-    lax.fori_loop(0, 7, one_chunk, 0)
-    local(0)
-    merge_step(0)
-
-    total = ms[0]
-    inverse = 1.0 / jnp.where(low_lanes, pltpu.roll(total, 64, 1), total)
-    inv_high = inverse.astype(BF16).astype(F32)
-    inv = jnp.where(low_lanes, inv_high, inverse - inv_high).astype(BF16)
+    lax.fori_loop(0, 9, one_chunk, 0)
+
+    parts, _, a1, a2, s = incoming(0, 1)
+    weight = jnp.where(low_lanes, a2, a1) / s
+    weight_high = weight.astype(BF16).astype(F32)
+    ab = jnp.concatenate([weight_high, weight - weight_high], axis=0).astype(BF16)
     mixed = []
     for l in range(LATENT):
-        factor = dot(inv, ex[l])
+        cols = slice(l * WIDTH, (l + 1) * WIDTH)
+        factor = dot(ab, ex[l])
+        factor = factor[:CHUNK] + factor[CHUNK:]
+        received = jnp.concatenate([rpart[0, 0, 0, :, cols], rpart[1, 0, 1, :, cols]], axis=0)
         mixed.append(
-            (part[0, :, l * WIDTH:(l + 1) * WIDTH].astype(F32)
-             * (factor[:, :WIDTH] + factor[:, WIDTH:])).astype(BF16)
+            (factor[:, :WIDTH] * received.astype(F32)
+             + factor[:, WIDTH:] * part[0, :, cols].astype(F32)).astype(BF16)
         )
     local_copies[8].wait()
     projected = dot(jnp.concatenate(mixed, axis=0), outw[...])
@@ -448,25 +465,22 @@
             device_id=member_dev(j), device_id_type=MESH,
         )
 
-    def pair_send(j, carry):
+    order = (1, 3, 5, 4, 7, 6, 2)
+    for j in order:
         pair_copy(j, member).start()
-        return carry
-
-    def pair_wait(j, carry):
-        pair_copy(j, mod(member + 8 - j, 8)).wait_recv()
-        return carry
-
-    lax.fori_loop(1, 8, pair_send, 0)
-    lax.fori_loop(1, 8, pair_wait, 0)
+    for j in order:
+        other = (flip(ylo, j // 4) * 2 + flip(core, (j // 2) % 2)) * 2 + flip(yhi, j % 2)
+        pair_copy(j, other).wait_recv()
     by_dest = dot(chosen[...], pairs[...].reshape(128, 2 * WIDTH))
     for k in range(16):
         table_f[:, k, :] = by_dest[(k // 8) * NVAR:(k // 8 + 1) * NVAR, (k % 8) * 128:(k % 8 + 1) * 128]
     table_b[...] = table_f[...].astype(BF16)
 
-    def row_copy(j):
+    def row_copy(i):
+        to_z, to_x = place_off(i)
         return pltpu.make_async_remote_copy(
-            src_ref=table_b.at[mod(place + j, NVAR)], dst_ref=rows.at[j], send_sem=ts.at[j],
-            recv_sem=tr.at[j], device_id=place_dev(j), device_id_type=MESH,
+            src_ref=table_b.at[to_z * 4 + to_x], dst_ref=rows.at[i], send_sem=ts.at[i],
+            recv_sem=tr.at[i], device_id=(to_z * GROUP + g, to_x * 2 + yhi), device_id_type=MESH,
         )
 
     def row_send(j, carry):
@@ -477,44 +491,42 @@
         row_copy(j).wait_recv()
         return carry
 
-    lax.fori_loop(1, NVAR, row_send, 0)
-    rows[0] = table_b[place]
-    lax.fori_loop(1, NVAR, row_wait, 0)
+    lax.fori_loop(0, NVAR - 1, row_send, 0)
+    rows[NVAR - 1] = table_b[z * 4 + x]
+    for copy in sends:
+        copy.wait_send()
+    for j in range(4):
+        forward_x(j, (right, left)[j % 2]).wait_send()
+    for j in range(6):
+        forward_core(0, j).wait_send()
+        forward_core(1, j).wait_send()
+
+    def ring_over(i, carry):
+        dr = mod(i, 2)
+        half = mod(div(i, 2), 2)
+        d = 1 + div(i, 4)
+
+        @pl.when((d < 4) | (half == dr))
+        def _():
+            for copy in ring_copies(dr, d, half):
+                copy.wait_send()
+
+        return carry
+
+    for j in order:
+        pair_copy(j, member).wait_send()
+
+    def row_over(j, carry):
+        row_copy(j).wait_send()
+        return carry
+
+    lax.fori_loop(0, 16, ring_over, 0)
+    lax.fori_loop(0, NVAR - 1, row_over, 0)
+    lax.fori_loop(0, NVAR - 1, row_wait, 0)
     total = jnp.sum(rows[...].astype(F32), axis=0) / count
     for l in range(LATENT):
         for k in range(4):
             means[0, l:l + 1, k * 128:(k + 1) * 128] = total[l * 4 + k:l * 4 + k + 1, :]
-
-    for copy in sends:
-        copy.wait_send()
-    for j in range(4):
-        forward_x(j, right).wait_send()
-        forward_core(0, j).wait_send()
-        forward_core(1, j).wait_send()
-
-    def ring_over(i, carry):
-        dr = mod(i, 2)
-        half = mod(div(i, 2), 2)
-        d = 1 + div(i, 4)
-
-        @pl.when((d < 4) | (half == dr))
-        def _():
-            for copy in ring_copies(dr, d, half):
-                copy.wait_send()
-
-        return carry
-
-    def pair_over(j, carry):
-        pair_copy(j, member).wait_send()
-        return carry
-
-    def row_over(j, carry):
-        row_copy(j).wait_send()
-        return carry
-
-    lax.fori_loop(0, 16, ring_over, 0)
-    lax.fori_loop(1, 8, pair_over, 0)
-    lax.fori_loop(1, NVAR, row_over, 0)
 
 
 def shards(fields, stem_in, stem_out, level_ids, level_table, latent_query, kv_weight, out_weight, region_ids):
@@ -559,7 +571,7 @@
             dma((9,)),
             dma((3,)), dma((3,)),
             dma((3,)), dma((3,)),
-            dma((6,)), dma((GROUP, 2, 4)), dma((4,)), dma((2, 4)),
+            dma((12,)), dma((GROUP, 2, 6)), dma((4,)), dma((2, 6)),
             dma((2, 4, 2)), dma((2, 4, 2)),
             dma((2, 4, 2)), dma((2, 4, 2)),
             dma((8,)), dma((8,)),

time: 72.5 us -> 69.2 us (0.954); the launches traced: 71.7 us -> 69.1 us
  Pallas kernels: 68.6 us -> 66 us
    pallas_call x1, Pallas kernels: 68.6 us -> 66 us  [shards(): pl.pallas_call(kernel, out_shape=(jax.ShapeDtypeStruct((CHUNK, FLAT), BF1...]
where the time goes in v2:
time: 69.2 us; the launch traced here: 69.1 us
  Pallas kernels  66 us (95%)
  local copies, waits for them, and re-layouts  2.44 us (4%)
    pallas_call x1, Pallas kernels, shards(): pl.pallas_call(kernel, out_shape=(jax.ShapeDtypeStruct((CHUNK, FLAT), BF1...  66 us
    reshape x1, local copies, waits for them, and re-layouts, shards(): return (lat.reshape(2, 32, LATENT, WIDTH), means)  1.84 us

profile of v2, /device:TPU:1, one launch (start us, length us, event | category | flops | bytes accessed | tf_op | source)
XLA Modules:
  0.0 69.1 jit_solution(17965399750169274267)
XLA Ops:
  0.6 66.0 %window.1 = (bf16[64,2048]{1,0:T(8,128)(2,1)}, f32[1,4,512]{2,1,0:T(4,128)}) custom-call(bf16[2,256,128]{2,1,0:T(8,128)(2,1)} %fields.1, bf16[2,16,512]{2,1,0:T(8,128)(2,1)} %stem_in.1, bf16[2,512,512]{2,1,0:T(8,128)(2,1)} %stem_out.1, s32[1,64]{1,0:T(1,128)} %bitcast.1, bf16[128,512]{1,0:T(8,128)(2,1)} %table_hbm.1, bf16[4,512]{1,0:T(4,128)(2,1)} %query_hbm.1, ...), custom_call_target="tpu_custom_call" | custom-call | tf_op jit(solution)/shard_map/window/pallas_call | solution.py:535
  66.7 0.0 copy-start
  66.7 1.8 %reshape.11 = bf16[2,32,4,512]{3,2,1,0:T(4,128)(2,1)} reshape(bf16[64,2048]{1,0:T(8,128)(2,1)} %get-tuple-element.4) | data formatting | bytes 524288 | tf_op jit(solution)/shard_map/reshape | solution.py:588
  68.5 0.0 copy-done
  68.5 0.6 copy.12
Async XLA Ops:
  66.7 1.9 %copy-start = (f32[1,4,512]{2,1,0:T(4,128)S(1)}, f32[1,4,512]{2,1,0:T(4,128)}, u32[]{:S(2)}) copy-start(f32[1,4,512]{2,1,0:T(4,128)} %get-tuple-element.9) | copy-start | bytes 24580

commit v3 on v2

--- a/solution.py
+++ b/solution.py
@@ -22,7 +22,7 @@
 CHUNK = 64
 HALF = 32
 LOG2E = 1.4426950408889634
-PIECES = ((0, 128), (128, 128), (256, 64), (320, 64), (384, 64), (448, 64))
+PIECES = ((0, 128), (128, 128), (256, 128), (384, 128))
 
 
 def iota(shape, axis):
@@ -138,22 +138,16 @@
     sends = [
         piece_copy(stem_out, 2, odd_x, 0, ws.at[0], next_dev),
         piece_copy(stem_out, 2, odd_x, 1, ws.at[1], prev_dev),
-        piece_copy(stem_out, 2, odd_x, 2, ws.at[2], next_dev),
-        piece_copy(stem_out, 2, odd_x, 3, ws.at[3], prev_dev),
-        whole_copy(0, ws.at[10]),
+        whole_copy(0, ws.at[6]),
         stem_copy(0, core_dev),
         stem_copy(1, (base + g_y, band_far)),
         stem_copy(2, (base + g_diag, band_far)),
-        whole_copy(1, ws.at[11]),
+        whole_copy(1, ws.at[7]),
     ]
     later = [
         pixel_copy(0, g_core, core_dev),
         pixel_copy(1, g_y, (base + g_y, bi)),
         pixel_copy(2, g_diag, (base + g_diag, bi)),
-        piece_copy(stem_out, 2, odd_x, 4, ws.at[4], next_dev),
-        piece_copy(stem_out, 2, odd_x, 5, ws.at[5], prev_dev),
-        piece_copy(stem_out, 2, 1 - odd_x, 4, ws.at[6], next_dev),
-        piece_copy(stem_out, 2, 1 - odd_x, 5, ws.at[7], prev_dev),
     ]
     for copy in sends:
         copy.start()
@@ -163,7 +157,13 @@
         pown[k] = ff[:, :, k].reshape(2 * NZ * 8, 128).astype(BF16)
     for copy in later:
         copy.start()
-    sends = sends + later
+    held = [
+        piece_copy(stem_out, 2, odd_x, 2, ws.at[2], next_dev),
+        piece_copy(stem_out, 2, odd_x, 3, ws.at[3], prev_dev),
+        piece_copy(stem_out, 2, 1 - odd_x, 2, ws.at[4], next_dev),
+        piece_copy(stem_out, 2, 1 - odd_x, 3, ws.at[5], prev_dev),
+    ]
+    sends = sends + later + held
     pbuf[0] = pown[g]
 
     def forward_x(j, target):
@@ -274,33 +274,40 @@
     def second_matrix(t):
         s, u = which(t)
 
+        @pl.when(t == 1)
+        def _():
+            for copy in held[:2]:
+                copy.start()
+
         @pl.when(t == 2)
         def _():
             whole_copy(0, ws.at[0]).wait_recv()
 
         @pl.when(t == 3)
         def _():
+            for j in range(2):
+                arrived(2, odd_x, j)
+                forward_x(j, (right, left)[j]).start()
+            for copy in held[2:]:
+                copy.start()
+            take_rest(odd_x, range(2))
+            whole_copy(1, ws.at[0]).wait_recv()
+
+        @pl.when(t == 4)
+        def _():
+            for j in (2, 3):
+                arrived(2, odd_x, j)
+            take_rest(odd_x, (2, 3))
+
+        @pl.when(t == 6)
+        def _():
             for j in range(4):
-                arrived(2, odd_x, j)
-                forward_x(j, (right, left)[j % 2]).start()
-            take_rest(odd_x, range(4))
-            whole_copy(1, ws.at[0]).wait_recv()
-
-        @pl.when(t == 4)
-        def _():
-            for j in (4, 5):
-                arrived(2, odd_x, j)
-            take_rest(odd_x, (4, 5))
-
-        @pl.when(t == 6)
-        def _():
-            for j in range(6):
                 arrived(2, 1 - odd_x, j)
                 forward_core(1 - odd_x, j).start()
 
         @pl.when((t == 5) | (t == 7))
         def _():
-            for j in range(6):
+            for j in range(4):
                 arrived(3, u, j)
 
         tokens = dot(normed[t], wbuf[s, u]).astype(BF16).astype(F32)
@@ -495,9 +502,9 @@
     rows[NVAR - 1] = table_b[z * 4 + x]
     for copy in sends:
         copy.wait_send()
+    for j in range(2):
+        forward_x(j, (right, left)[j]).wait_send()
     for j in range(4):
-        forward_x(j, (right, left)[j % 2]).wait_send()
-    for j in range(6):
         forward_core(0, j).wait_send()
         forward_core(1, j).wait_send()
 
@@ -571,7 +578,7 @@
             dma((9,)),
             dma((3,)), dma((3,)),
             dma((3,)), dma((3,)),
-            dma((12,)), dma((GROUP, 2, 6)), dma((4,)), dma((2, 6)),
+            dma((8,)), dma((GROUP, 2, 4)), dma((2,)), dma((2, 4)),
             dma((2, 4, 2)), dma((2, 4, 2)),
             dma((2, 4, 2)), dma((2, 4, 2)),
             dma((8,)), dma((8,)),

time: 69.2 us -> 67.7 us (0.978)
  Pallas kernels: 66 us -> 64.4 us
    pallas_call x1, Pallas kernels: 66 us -> 64.4 us  [shards(): pl.pallas_call(kernel, out_shape=(jax.ShapeDtypeStruct((CHUNK, FLAT), BF1...]
where the time goes in v3:
time: 67.7 us; the launch traced here: 67.5 us
  Pallas kernels  64.4 us (95%)
  local copies, waits for them, and re-layouts  2.44 us (4%)
    pallas_call x1, Pallas kernels, shards(): pl.pallas_call(kernel, out_shape=(jax.ShapeDtypeStruct((CHUNK, FLAT), BF1...  64.4 us
    reshape x1, local copies, waits for them, and re-layouts, shards(): return (lat.reshape(2, 32, LATENT, WIDTH), means)  1.84 us

profile of v3, /device:TPU:1, one launch (start us, length us, event | category | flops | bytes accessed | tf_op | source)
XLA Modules:
  0.0 67.5 jit_solution(13155764624688249022)
XLA Ops:
  0.6 64.4 %window.1 = (bf16[64,2048]{1,0:T(8,128)(2,1)}, f32[1,4,512]{2,1,0:T(4,128)}) custom-call(bf16[2,256,128]{2,1,0:T(8,128)(2,1)} %fields.1, bf16[2,16,512]{2,1,0:T(8,128)(2,1)} %stem_in.1, bf16[2,512,512]{2,1,0:T(8,128)(2,1)} %stem_out.1, s32[1,64]{1,0:T(1,128)} %bitcast.1, bf16[128,512]{1,0:T(8,128)(2,1)} %table_hbm.1, bf16[4,512]{1,0:T(4,128)(2,1)} %query_hbm.1, ...), custom_call_target="tpu_custom_call" | custom-call | tf_op jit(solution)/shard_map/window/pallas_call | solution.py:542
  65.1 0.0 copy-start
  65.1 1.8 %reshape.11 = bf16[2,32,4,512]{3,2,1,0:T(4,128)(2,1)} reshape(bf16[64,2048]{1,0:T(8,128)(2,1)} %get-tuple-element.4) | data formatting | bytes 524288 | tf_op jit(solution)/shard_map/reshape | solution.py:595
  66.9 0.0 copy-done
  66.9 0.6 copy.12
Async XLA Ops:
  65.1 1.9 %copy-start = (f32[1,4,512]{2,1,0:T(4,128)S(1)}, f32[1,4,512]{2,1,0:T(4,128)}, u32[]{:S(2)}) copy-start(f32[1,4,512]{2,1,0:T(4,128)} %get-tuple-element.9) | copy-start | bytes 24580

commit v4 on v3

--- a/solution.py
+++ b/solution.py
@@ -343,7 +343,7 @@
         start = pl.multiple_of(half * HALF, HALF)
         return (
             pltpu.make_async_remote_copy(
-                src_ref=ms.at[off, pl.ds(start, HALF), :], dst_ref=rms.at[dr, d - 1, half],
+                src_ref=ms.at[off, pl.ds(pl.multiple_of(half * 16, 16), 16), :], dst_ref=rms.at[dr, d - 1, half],
                 send_sem=mss.at[dr, d - 1, half], recv_sem=msr.at[dr, d - 1, half],
                 device_id=target, device_id_type=MESH,
             ),
@@ -358,14 +358,24 @@
         for copy in ring_copies(dr, d, half):
             copy.start()
 
+    def put_level(off, half, level):
+        ms[off, pl.ds(pl.multiple_of(half * 16, 16), 16), :] = jnp.where(low_lanes[:16], level[:16], level[16:])
+
+    def both_lanes(packed):
+        turned = pltpu.roll(packed, 64, 1)
+        low = low_lanes[:16]
+        return [jnp.where(low, packed, turned), jnp.where(low, turned, packed)]
+
     def local(off):
         start = pl.multiple_of(mod(z + off, NZ) * CHUNK, CHUNK)
         nb = normed[:, pl.ds(start, CHUNK), :].reshape(8 * CHUNK, WIDTH)
         scores = dot(nb, qk[...])
         scores = (scores + pltpu.roll(scores, 64, 1)).reshape(8, CHUNK, 128)
-        top = jnp.ceil(jnp.max(scores, axis=0))
-        p = jnp.exp2(scores - top[None])
-        ms[off] = jnp.where(low_lanes, top, jnp.sum(p, axis=0))
+        top = jnp.max(scores, axis=0)
+        level = top + jnp.log2(jnp.sum(jnp.exp2(scores - top[None]), axis=0))
+        p = jnp.exp2(scores - jnp.ceil(level)[None])
+        put_level(off, 0, level[:HALF])
+        put_level(off, 1, level[HALF:])
         pb = p.astype(BF16).reshape(8 * CHUNK, 128)
         values = dot(nb, kvw[:, WIDTH:])
         for l in range(LATENT):
@@ -384,25 +394,24 @@
         parts = []
         for dr, h in ((0, 1 - i), (1, i)):
             parts.append((dr, h, offset(dr, d), pl.ds(pl.multiple_of(h * HALF, HALF), HALF)))
-        mine = jnp.concatenate([ms[off, at, :] for _, _, off, at in parts], axis=0)
-        other = jnp.concatenate([rms[dr, d, h] for dr, h, _, _ in parts], axis=0)
-        mine_r = pltpu.roll(mine, 64, 1)
-        other_r = pltpu.roll(other, 64, 1)
-        m1 = jnp.where(low_lanes, mine, mine_r)
-        s1 = jnp.where(low_lanes, mine_r, mine)
-        m2 = jnp.where(low_lanes, other, other_r)
-        s2 = jnp.where(low_lanes, other_r, other)
-        m = jnp.maximum(m1, m2)
-        a1 = jnp.exp2(m1 - m)
-        a2 = jnp.exp2(m2 - m)
-        return parts, m, a1, a2, a1 * s1 + a2 * s2
+        mine, other = [], []
+        for dr, h, off, _ in parts:
+            mine += both_lanes(ms[off, pl.ds(pl.multiple_of(h * 16, 16), 16), :])
+            other += both_lanes(rms[dr, d, h])
+        level1 = jnp.concatenate(mine, axis=0)
+        level2 = jnp.concatenate(other, axis=0)
+        m1 = jnp.ceil(level1)
+        m2 = jnp.ceil(level2)
+        top = jnp.maximum(m1, m2)
+        level = top + jnp.log2(jnp.exp2(level1 - top) + jnp.exp2(level2 - top))
+        m = jnp.ceil(level)
+        return parts, level, jnp.exp2(m1 - m), jnp.exp2(m2 - m)
 
     def merge(d, i):
-        parts, m, a1, a2, s = incoming(d, i)
-        new = jnp.where(low_lanes, m, s)
+        parts, level, a1, a2 = incoming(d, i)
         ab = jnp.where(low_lanes, a2, a1).astype(BF16)
-        for k, (_, _, off, at) in enumerate(parts):
-            ms[off, at, :] = new[k * HALF:(k + 1) * HALF]
+        for k, (_, h, off, _) in enumerate(parts):
+            put_level(off, h, level[k * HALF:(k + 1) * HALF])
         for l in range(LATENT):
             cols = slice(l * WIDTH, (l + 1) * WIDTH)
             factor = dot(ab, ex[l])
@@ -440,8 +449,8 @@
 
     lax.fori_loop(0, 9, one_chunk, 0)
 
-    parts, _, a1, a2, s = incoming(0, 1)
-    weight = jnp.where(low_lanes, a2, a1) / s
+    _, level, a1, a2 = incoming(0, 1)
+    weight = jnp.where(low_lanes, a2, a1) * jnp.exp2(jnp.ceil(level) - level)
     weight_high = weight.astype(BF16).astype(F32)
     ab = jnp.concatenate([weight_high, weight - weight_high], axis=0).astype(BF16)
     mixed = []
@@ -567,9 +576,9 @@
             pltpu.VMEM((WIDTH, 128), BF16),
             pltpu.VMEM((LATENT, 128, 2 * WIDTH), BF16),
             pltpu.VMEM((NZ, CHUNK, FLAT), BF16),
-            pltpu.VMEM((NZ, CHUNK, 128), F32),
+            pltpu.VMEM((NZ, HALF, 128), F32),
             pltpu.VMEM((2, 4, 2, HALF, FLAT), BF16),
-            pltpu.VMEM((2, 4, 2, HALF, 128), F32),
+            pltpu.VMEM((2, 4, 2, 16, 128), F32),
             pltpu.VMEM((2 * NVAR, 128), BF16),
             pltpu.VMEM((8, 16, 2 * WIDTH), BF16),
             pltpu.VMEM((NVAR, 16, 128), F32),

time: 67.7 us -> 66.9 us (0.988)
  Pallas kernels: 64.4 us -> 63.6 us
    pallas_call x1, Pallas kernels: 64.4 us -> 63.6 us  [shards(): pl.pallas_call(kernel, out_shape=(jax.ShapeDtypeStruct((CHUNK, FLAT), BF1...]
where the time goes in v4:
time: 66.9 us; the launch traced here: 66.7 us
  Pallas kernels  63.6 us (95%)
  local copies, waits for them, and re-layouts  2.44 us (4%)
    pallas_call x1, Pallas kernels, shards(): pl.pallas_call(kernel, out_shape=(jax.ShapeDtypeStruct((CHUNK, FLAT), BF1...  63.6 us
    reshape x1, local copies, waits for them, and re-layouts, shards(): return (lat.reshape(2, 32, LATENT, WIDTH), means)  1.84 us

profile of v4, /device:TPU:1, one launch (start us, length us, event | category | flops | bytes accessed | tf_op | source)
XLA Modules:
  0.0 66.7 jit_solution(3574047994956894397)
XLA Ops:
  0.6 63.6 %window.1 = (bf16[64,2048]{1,0:T(8,128)(2,1)}, f32[1,4,512]{2,1,0:T(4,128)}) custom-call(bf16[2,256,128]{2,1,0:T(8,128)(2,1)} %fields.1, bf16[2,16,512]{2,1,0:T(8,128)(2,1)} %stem_in.1, bf16[2,512,512]{2,1,0:T(8,128)(2,1)} %stem_out.1, s32[1,64]{1,0:T(1,128)} %bitcast.1, bf16[128,512]{1,0:T(8,128)(2,1)} %table_hbm.1, bf16[4,512]{1,0:T(4,128)(2,1)} %query_hbm.1, ...), custom_call_target="tpu_custom_call" | custom-call | tf_op jit(solution)/shard_map/window/pallas_call | solution.py:551
  64.3 0.0 copy-start
  64.3 1.8 %reshape.11 = bf16[2,32,4,512]{3,2,1,0:T(4,128)(2,1)} reshape(bf16[64,2048]{1,0:T(8,128)(2,1)} %get-tuple-element.4) | data formatting | bytes 524288 | tf_op jit(solution)/shard_map/reshape | solution.py:604
  66.1 0.0 copy-done
  66.1 0.6 copy.12
Async XLA Ops:
  64.3 1.9 %copy-start = (f32[1,4,512]{2,1,0:T(4,128)S(1)}, f32[1,4,512]{2,1,0:T(4,128)}, u32[]{:S(2)}) copy-start(f32[1,4,512]{2,1,0:T(4,128)} %get-tuple-element.9) | copy-start | bytes 24580

commit v5 on v4

--- a/solution.py
+++ b/solution.py
@@ -46,9 +46,9 @@
 
 
 def kernel(
-    fields, stem_in, stem_out, ids_hbm, table_hbm, query_hbm, kvw_hbm, outw_hbm, regions_hbm,
+    fields, stem_in, stem_out, ids_hbm, table_hbm, query, kvw_hbm, outw_hbm, regions_hbm,
     lat, means,
-    field_v, ids, table, query, kvw, outw, regions,
+    field_v, ids, table, kvw, outw, regions,
     pbuf, pown, sbuf, wbuf, fscr, lhs, tile, normed, emb, qk, ex,
     part, ms, rpart, rms, chosen, pairs, table_f, table_b, rows,
     lsem, ps, pr, ss, sr, ws, wr, xs, fs, os, orr, mss, msr, cs, cr, ts, tr,
@@ -99,7 +99,7 @@
         pltpu.make_async_copy(src, dst, lsem.at[k])
         for k, (src, dst) in enumerate((
             (fields, field_v), (stem_out, wbuf.at[0]), (stem_in, sbuf.at[0]), (ids_hbm, ids),
-            (table_hbm, table), (query_hbm, query), (kvw_hbm, kvw), (regions_hbm, regions),
+            (table_hbm, table), (kvw_hbm, kvw), (regions_hbm, regions),
             (outw_hbm, outw),
         ))
     ]
@@ -195,7 +195,7 @@
         copy.wait()
     onehot = (iota((128, 64), 0) == ids[...]).astype(F32)
     emb[...] = dot(onehot.T.astype(BF16), table[...])
-    for copy in local_copies[5:8]:
+    for copy in local_copies[5:7]:
         copy.wait()
     qf = query[...].astype(F32)
     heads = iota((HEADS, WIDTH), 0) == div(iota((HEADS, WIDTH), 1), HEAD)
@@ -463,7 +463,7 @@
             (factor[:, :WIDTH] * received.astype(F32)
              + factor[:, WIDTH:] * part[0, :, cols].astype(F32)).astype(BF16)
         )
-    local_copies[8].wait()
+    local_copies[7].wait()
     projected = dot(jnp.concatenate(mixed, axis=0), outw[...])
     sums = []
     for l in range(LATENT):
@@ -554,13 +554,12 @@
             jax.ShapeDtypeStruct((CHUNK, FLAT), BF16),
             jax.ShapeDtypeStruct((1, LATENT, WIDTH), F32),
         ),
-        in_specs=[pl.BlockSpec(memory_space=pl.ANY)] * 9,
+        in_specs=[vmem if k == 5 else pl.BlockSpec(memory_space=pl.ANY) for k in range(9)],
         out_specs=(vmem, vmem),
         scratch_shapes=[
             pltpu.VMEM((2, 256, 128), BF16),
             pltpu.VMEM((1, 64), I32),
             pltpu.VMEM((128, WIDTH), BF16),
-            pltpu.VMEM((LATENT, WIDTH), BF16),
             pltpu.VMEM((WIDTH, 2 * WIDTH), BF16),
             pltpu.VMEM((WIDTH, WIDTH), BF16),
             pltpu.VMEM((32, 128), I32),
@@ -584,7 +583,7 @@
             pltpu.VMEM((NVAR, 16, 128), F32),
             pltpu.VMEM((NVAR, 16, 128), BF16),
             pltpu.VMEM((NVAR, 16, 128), BF16),
-            dma((9,)),
+            dma((8,)),
             dma((3,)), dma((3,)),
             dma((3,)), dma((3,)),
             dma((8,)), dma((GROUP, 2, 4)), dma((2,)), dma((2, 4)),

time: 66.9 us -> 67.5 us (level)
  no operation moved by 1% of the time
where the time goes in v5:
time: 67.5 us; the launch traced here: 67.3 us
  Pallas kernels  64.2 us (95%)
  local copies, waits for them, and re-layouts  2.44 us (4%)
    pallas_call x1, Pallas kernels, shards(): pl.pallas_call(kernel, out_shape=(jax.ShapeDtypeStruct((CHUNK, FLAT), BF1...  64.2 us
    reshape x1, local copies, waits for them, and re-layouts, shards(): return (lat.reshape(2, 32, LATENT, WIDTH), means)  1.84 us

profile of v5, /device:TPU:1, one launch (start us, length us, event | category | flops | bytes accessed | tf_op | source)
XLA Modules:
  0.0 67.3 jit_solution(12596830668307292682)
XLA Ops:
  0.6 64.2 %window.1 = (bf16[64,2048]{1,0:T(8,128)(2,1)}, f32[1,4,512]{2,1,0:T(4,128)}) custom-call(bf16[2,256,128]{2,1,0:T(8,128)(2,1)} %fields.1, bf16[2,16,512]{2,1,0:T(8,128)(2,1)} %stem_in.1, bf16[2,512,512]{2,1,0:T(8,128)(2,1)} %stem_out.1, s32[1,64]{1,0:T(1,128)} %bitcast.1, bf16[128,512]{1,0:T(8,128)(2,1)} %table_hbm.1, bf16[4,512]{1,0:T(4,128)(2,1)} %query.1, ...), custom_call_target="tpu_custom_call" | custom-call | tf_op jit(solution)/shard_map/window/pallas_call | solution.py:551
  64.9 0.0 copy-start
  64.9 1.8 %reshape.11 = bf16[2,32,4,512]{3,2,1,0:T(4,128)(2,1)} reshape(bf16[64,2048]{1,0:T(8,128)(2,1)} %get-tuple-element.4) | data formatting | bytes 524288 | tf_op jit(solution)/shard_map/reshape | solution.py:603
  66.7 0.0 copy-done
  66.7 0.6 copy.12
Async XLA Ops:
  64.9 1.9 %copy-start = (f32[1,4,512]{2,1,0:T(4,128)S(1)}, f32[1,4,512]{2,1,0:T(4,128)}, u32[]{:S(2)}) copy-start(f32[1,4,512]{2,1,0:T(4,128)} %get-tuple-element.9) | copy-start | bytes 24580

commit v6 on v4

--- a/solution.py
+++ b/solution.py
@@ -187,58 +187,10 @@
         (div(iota((512, 128), 0), 128) == div(iota((512, 128), 1), 4))
         & (mod(iota((512, 128), 0), 4) == mod(iota((512, 128), 1), 4))
     ).astype(F32).astype(BF16)
-    for l in range(LATENT):
-        lane = iota((128, 1024), 1)
-        want = div(mod(lane, WIDTH), HEAD) + l * HEADS + div(lane, WIDTH) * 64
-        ex[l] = (iota((128, 1024), 0) == want).astype(F32).astype(BF16)
     for copy in local_copies[3:5]:
         copy.wait()
     onehot = (iota((128, 64), 0) == ids[...]).astype(F32)
     emb[...] = dot(onehot.T.astype(BF16), table[...])
-    for copy in local_copies[5:8]:
-        copy.wait()
-    qf = query[...].astype(F32)
-    heads = iota((HEADS, WIDTH), 0) == div(iota((HEADS, WIDTH), 1), HEAD)
-    qmat = jnp.concatenate(
-        [jnp.where(heads, jnp.broadcast_to(qf[l:l + 1], (HEADS, WIDTH)), 0.0) for l in range(LATENT)],
-        axis=0,
-    ).astype(BF16)
-    folded = dot_nt(qmat, kvw[:, :WIDTH]) * (LOG2E / HEAD**0.5)
-    high = folded.astype(BF16).astype(F32)
-    qk[...] = jnp.concatenate([high, folded - high], axis=0).T.astype(BF16)
-
-    ones = jnp.ones((128, 128), F32)
-    same_tile = div(iota((128, 128), 0), 16) == div(iota((128, 128), 1), 16)
-    slot_row = iota((128, 128), 0)
-    tile_lane = div(iota((128, 128), 1), 16)
-    dest = iota((NVAR, 128), 0)
-    dest_region = (div(dest, 4) * GROUP + g) * NBAND + mod(dest, 4) * 2 + yhi
-    picked = jnp.zeros((NVAR, 128), F32)
-
-    def slots(row):
-        across = row.astype(F32) * ones
-        below = jnp.where((across.T < across) & same_tile, 0.5, 0.0)
-        return jnp.sum(below, axis=0, keepdims=True).astype(I32)
-
-    for k in range(GROUP):
-        row = regions[pl.ds(base + k, 1), :]
-        hit = (slots(row) == mod(slot_row, 8)) & (div(slot_row, 32) == k) & (
-            tile_lane == x * 2 + mod(div(slot_row, 16), 2)
-        )
-        in_region = (row == dest_region).astype(F32).astype(BF16)
-        picked = picked + dot_nt(in_region, jnp.where(hit, 0.5, 0.0).astype(BF16))
-    upper = mod(div(iota((NVAR, 128), 1), 8), 2) == 1
-    chosen[...] = jnp.concatenate(
-        [jnp.where(upper, 0.0, picked), jnp.where(upper, picked, 0.0)], axis=0
-    ).astype(BF16)
-    own_row = regions[pl.ds(vi, 1), :]
-    own_hit = (slots(own_row) == iota((8, 128), 0)) & (div(iota((8, 128), 1), 16) == bi)
-    cell = div(mod(iota((128, CHUNK), 1), HALF), 2)
-    average = jnp.where(mod(iota((128, CHUNK), 0), 16) == cell, 0.25, 0.0).astype(BF16)
-    pair_mean = dot(own_hit.astype(F32).astype(BF16), average).astype(BF16)
-    region = vi * NBAND + bi
-    count = jnp.sum((regions[...] == region).astype(F32))
-
     local_copies[1].wait()
     local_copies[2].wait()
     patch_mask = div(iota((HALF, 128), 1), 4) == iota((HALF, 128), 0)
@@ -250,6 +202,25 @@
             (1 - late) * div(t, 2) + late * (2 + mod(t, 2)),
             (1 - late) * mod(t, 2) + late * (odd_x + second - 2 * odd_x * second),
         )
+
+    def constants():
+        for l in range(LATENT):
+            lane = iota((128, 1024), 1)
+            want = div(mod(lane, WIDTH), HEAD) + l * HEADS + div(lane, WIDTH) * 64
+            ex[l] = (iota((128, 1024), 0) == want).astype(F32).astype(BF16)
+        for copy in local_copies[5:7]:
+            copy.wait()
+        qf = query[...].astype(F32)
+        heads = iota((HEADS, WIDTH), 0) == div(iota((HEADS, WIDTH), 1), HEAD)
+        qmat = jnp.concatenate(
+            [jnp.where(heads, jnp.broadcast_to(qf[l:l + 1], (HEADS, WIDTH)), 0.0) for l in range(LATENT)],
+            axis=0,
+        ).astype(BF16)
+        folded = dot_nt(qmat, kvw[:, :WIDTH]) * (LOG2E / HEAD**0.5)
+        high = folded.astype(BF16).astype(F32)
+        qk[...] = jnp.concatenate([high, folded - high], axis=0).T.astype(BF16)
+
+    constants()
 
     def first_matrix(t):
         s, u = which(t)
@@ -269,7 +240,7 @@
         pixels = dot(lhs[...], tile[...]).astype(BF16)[:, :16]
         h = dot(pixels, sbuf[s, u])
         stem = 0.5 * h * (1.0 + jnp.tanh(0.7978845608028654 * (h + 0.044715 * (h * h * h))))
-        normed[t] = stem.astype(BF16)
+        normed[t + div(t, 7)] = stem.astype(BF16)
 
     def second_matrix(t):
         s, u = which(t)
@@ -310,7 +281,9 @@
             for j in range(4):
                 arrived(3, u, j)
 
-        tokens = dot(normed[t], wbuf[s, u]).astype(BF16).astype(F32)
+    def project(t, src, at):
+        s, u = which(t)
+        tokens = dot(normed[src, at, :], wbuf[s, u]).astype(BF16).astype(F32)
         src_g = mod(s, 2)
         src_core = core + src_g - 2 * core * src_g
         up = div(s, 2)
@@ -320,7 +293,7 @@
         centre = jnp.mean(keyed, axis=-1, keepdims=True)
         away = keyed - centre
         spread = jnp.mean(away * away, axis=-1, keepdims=True)
-        normed[t] = (away * lax.rsqrt(spread + 1e-05)).astype(BF16)
+        normed[t, at, :] = (away * lax.rsqrt(spread + 1e-05)).astype(BF16)
 
     def one_variable(t, carry):
         @pl.when(t < 8)
@@ -331,9 +304,15 @@
         def _():
             second_matrix(t - 1)
 
+            @pl.when(t < 8)
+            def _():
+                project(t - 1, t - 1, pl.ds(0, 512))
+
         return carry
 
     lax.fori_loop(0, 9, one_variable, 0)
+    last = jnp.int32(7)
+    project(last, 8, pl.ds(pl.multiple_of(mod(z + 4, NZ) * CHUNK, CHUNK), CHUNK))
 
     low_lanes = iota((CHUNK, 128), 1) < 64
 
@@ -368,7 +347,7 @@
 
     def local(off):
         start = pl.multiple_of(mod(z + off, NZ) * CHUNK, CHUNK)
-        nb = normed[:, pl.ds(start, CHUNK), :].reshape(8 * CHUNK, WIDTH)
+        nb = normed[:8, pl.ds(start, CHUNK), :].reshape(8 * CHUNK, WIDTH)
         scores = dot(nb, qk[...])
         scores = (scores + pltpu.roll(scores, 64, 1)).reshape(8, CHUNK, 128)
         top = jnp.max(scores, axis=0)
@@ -435,6 +414,7 @@
         def _():
             ring_send(0, 4, 0)
             ring_send(1, 4, 1)
+            project(last, 8, pl.ds(0, 512))
 
         @pl.when(k > 2)
         def _():
@@ -448,6 +428,39 @@
         return carry
 
     lax.fori_loop(0, 9, one_chunk, 0)
+
+    local_copies[7].wait()
+    ones = jnp.ones((128, 128), F32)
+    same_tile = div(iota((128, 128), 0), 16) == div(iota((128, 128), 1), 16)
+    slot_row = iota((128, 128), 0)
+    tile_lane = div(iota((128, 128), 1), 16)
+    dest = iota((NVAR, 128), 0)
+    dest_region = (div(dest, 4) * GROUP + g) * NBAND + mod(dest, 4) * 2 + yhi
+    picked = jnp.zeros((NVAR, 128), F32)
+
+    def slots(row):
+        across = row.astype(F32) * ones
+        below = jnp.where((across.T < across) & same_tile, 0.5, 0.0)
+        return jnp.sum(below, axis=0, keepdims=True).astype(I32)
+
+    for k in range(GROUP):
+        row = regions[pl.ds(base + k, 1), :]
+        hit = (slots(row) == mod(slot_row, 8)) & (div(slot_row, 32) == k) & (
+            tile_lane == x * 2 + mod(div(slot_row, 16), 2)
+        )
+        in_region = (row == dest_region).astype(F32).astype(BF16)
+        picked = picked + dot_nt(in_region, jnp.where(hit, 0.5, 0.0).astype(BF16))
+    upper = mod(div(iota((NVAR, 128), 1), 8), 2) == 1
+    chosen[...] = jnp.concatenate(
+        [jnp.where(upper, 0.0, picked), jnp.where(upper, picked, 0.0)], axis=0
+    ).astype(BF16)
+    own_row = regions[pl.ds(vi, 1), :]
+    own_hit = (slots(own_row) == iota((8, 128), 0)) & (div(iota((8, 128), 1), 16) == bi)
+    cell = div(mod(iota((128, CHUNK), 1), HALF), 2)
+    average = jnp.where(mod(iota((128, CHUNK), 0), 16) == cell, 0.25, 0.0).astype(BF16)
+    pair_mean = dot(own_hit.astype(F32).astype(BF16), average).astype(BF16)
+    region = vi * NBAND + bi
+    count = jnp.sum((regions[...] == region).astype(F32))
 
     _, level, a1, a2 = incoming(0, 1)
     weight = jnp.where(low_lanes, a2, a1) * jnp.exp2(jnp.ceil(level) - level)
@@ -468,7 +481,7 @@
     sums = []
     for l in range(LATENT):
         cols = slice(l * WIDTH, (l + 1) * WIDTH)
-        out = (projected[l * CHUNK:(l + 1) * CHUNK] + qf[l:l + 1]).astype(BF16)
+        out = (projected[l * CHUNK:(l + 1) * CHUNK] + query[l:l + 1].astype(F32)).astype(BF16)
         lat[:, cols] = out
         sums.append(dot(pair_mean, out))
     pairs[member] = jnp.concatenate(
@@ -571,7 +584,7 @@
             pltpu.VMEM((CHUNK, 128), F32),
             pltpu.VMEM((512, 512), BF16),
             pltpu.VMEM((512, 128), BF16),
-            pltpu.VMEM((8, 512, WIDTH), BF16),
+            pltpu.VMEM((9, 512, WIDTH), BF16),
             pltpu.VMEM((64, WIDTH), F32),
             pltpu.VMEM((WIDTH, 128), BF16),
             pltpu.VMEM((LATENT, 128, 2 * WIDTH), BF16),

time: 66.9 us -> 66.5 us (level)
  no operation moved by 1% of the time
where the time goes in v6:
time: 66.5 us; the launch traced here: 66.4 us
  Pallas kernels  63.3 us (95%)
  local copies, waits for them, and re-layouts  2.44 us (4%)
    pallas_call x1, Pallas kernels, shards(): pl.pallas_call(kernel, out_shape=(jax.ShapeDtypeStruct((CHUNK, FLAT), BF1...  63.3 us
    reshape x1, local copies, waits for them, and re-layouts, shards(): return (lat.reshape(2, 32, LATENT, WIDTH), means)  1.84 us

profile of v6, /device:TPU:1, one launch (start us, length us, event | category | flops | bytes accessed | tf_op | source)
XLA Modules:
  0.0 66.4 jit_solution(13768226706490595315)
XLA Ops:
  0.6 63.3 %window.1 = (bf16[64,2048]{1,0:T(8,128)(2,1)}, f32[1,4,512]{2,1,0:T(4,128)}) custom-call(bf16[2,256,128]{2,1,0:T(8,128)(2,1)} %fields.1, bf16[2,16,512]{2,1,0:T(8,128)(2,1)} %stem_in.1, bf16[2,512,512]{2,1,0:T(8,128)(2,1)} %stem_out.1, s32[1,64]{1,0:T(1,128)} %bitcast.1, bf16[128,512]{1,0:T(8,128)(2,1)} %table_hbm.1, bf16[4,512]{1,0:T(4,128)(2,1)} %query_hbm.1, ...), custom_call_target="tpu_custom_call" | custom-call | tf_op jit(solution)/shard_map/window/pallas_call | solution.py:564
  63.9 0.0 copy-start
  63.9 1.8 %reshape.11 = bf16[2,32,4,512]{3,2,1,0:T(4,128)(2,1)} reshape(bf16[64,2048]{1,0:T(8,128)(2,1)} %get-tuple-element.4) | data formatting | bytes 524288 | tf_op jit(solution)/shard_map/reshape | solution.py:617
  65.8 0.0 copy-done
  65.8 0.6 copy.12
Async XLA Ops:
  63.9 1.9 %copy-start = (f32[1,4,512]{2,1,0:T(4,128)S(1)}, f32[1,4,512]{2,1,0:T(4,128)}, u32[]{:S(2)}) copy-start(f32[1,4,512]{2,1,0:T(4,128)} %get-tuple-element.9) | copy-start | bytes 24580

commit v7 on v6

--- a/solution.py
+++ b/solution.py
@@ -89,8 +89,8 @@
         return mod(z + da, NZ), mod(x + db, 4)
 
     barrier = pltpu.get_barrier_semaphore()
-    near = [member_dev(j) for j in range(1, 8)]
-    near += [(vi, mod(x + j, 4) * 2 + yhi) for j in range(1, 4)]
+    near = [member_dev(j) for j in (2, 4, 5, 6, 7)]
+    near += [right, left]
     near += [(mod(z + j, NZ) * GROUP + g, bi) for j in (1, NZ - 1)]
     for device in near:
         pl.semaphore_signal(barrier, inc=1, device_id=device, device_id_type=MESH)

time: 66.5 us -> 66.4 us (level)
  no operation moved by 1% of the time
where the time goes in v7:
time: 66.4 us; the launch traced here: 66.2 us
  Pallas kernels  63.2 us (95%)
  local copies, waits for them, and re-layouts  2.44 us (4%)
    pallas_call x1, Pallas kernels, shards(): pl.pallas_call(kernel, out_shape=(jax.ShapeDtypeStruct((CHUNK, FLAT), BF1...  63.2 us
    reshape x1, local copies, waits for them, and re-layouts, shards(): return (lat.reshape(2, 32, LATENT, WIDTH), means)  1.84 us

profile of v7, /device:TPU:1, one launch (start us, length us, event | category | flops | bytes accessed | tf_op | source)
XLA Modules:
  0.0 66.2 jit_solution(8732203833771509051)
XLA Ops:
  0.6 63.2 %window.1 = (bf16[64,2048]{1,0:T(8,128)(2,1)}, f32[1,4,512]{2,1,0:T(4,128)}) custom-call(bf16[2,256,128]{2,1,0:T(8,128)(2,1)} %fields.1, bf16[2,16,512]{2,1,0:T(8,128)(2,1)} %stem_in.1, bf16[2,512,512]{2,1,0:T(8,128)(2,1)} %stem_out.1, s32[1,64]{1,0:T(1,128)} %bitcast.1, bf16[128,512]{1,0:T(8,128)(2,1)} %table_hbm.1, bf16[4,512]{1,0:T(4,128)(2,1)} %query_hbm.1, ...), custom_call_target="tpu_custom_call" | custom-call | tf_op jit(solution)/shard_map/window/pallas_call | solution.py:564
  63.8 0.0 copy-start
  63.8 1.8 %reshape.11 = bf16[2,32,4,512]{3,2,1,0:T(4,128)(2,1)} reshape(bf16[64,2048]{1,0:T(8,128)(2,1)} %get-tuple-element.4) | data formatting | bytes 524288 | tf_op jit(solution)/shard_map/reshape | solution.py:617
  65.6 0.0 copy-done
  65.7 0.6 copy.12
Async XLA Ops:
  63.8 1.9 %copy-start = (f32[1,4,512]{2,1,0:T(4,128)S(1)}, f32[1,4,512]{2,1,0:T(4,128)}, u32[]{:S(2)}) copy-start(f32[1,4,512]{2,1,0:T(4,128)} %get-tuple-element.9) | copy-start | bytes 24580
